TPU v7x, 32 devices: a whole 2x2x4 slice. The times are simulated.
32 devices in a mesh: dp: 16 (over z, y, x), tp: 2 (over core).
Axes of the slice: x: 2, y: 2, z: 4, core: 2. Of those that a mesh axis runs over, the one named last changes fastest.
Arguments:
- hidden: bfloat16 [64, 256, 410], P('dp', 'tp'), may hold values from -6 to 6
- memory: bfloat16 [64, 256, 410], P('dp', 'tp'), may hold values from -6 to 6
- segment_length: int32 [64], P('dp'), may hold values from 1 to 256, as said below
- memory_length: int32 [64], P('dp'), may hold values from 0 to 256
- doc_reset: int32 [64, 256], P('dp'), may hold values from 0 to 1
- w_query: bfloat16 [410, 410], replicated, may hold values from -0.3125 to 0.3125
- w_key: bfloat16 [410, 410], replicated, may hold values from -0.3125 to 0.3125
- w_value: bfloat16 [410, 410], replicated, may hold values from -0.3125 to 0.3125
- w_pos: bfloat16 [410, 410], replicated, may hold values from -0.3125 to 0.3125
- bias_u: float32 [410], replicated, may hold values from -3 to 3
- bias_v: float32 [410], replicated, may hold values from -3 to 3
- w_out: bfloat16 [410, 410], replicated, may hold values from -1.25 to 1.25
- first_gain: float32 [410], replicated, may hold values from 0.5 to 1.5
- first_shift: float32 [410], replicated, may hold values from -2 to 2
- ffn_in: bfloat16 [410, 2100], P(None, 'tp'), may hold values from -0.3125 to 0.3125
- ffn_in_bias: bfloat16 [2100], P('tp'), may hold values from -3 to 3
- ffn_out: bfloat16 [2100, 410], P('tp'), may hold values from -0.125 to 0.125
- ffn_out_bias: float32 [410], replicated, may hold values from -2 to 2
- second_gain: float32 [410], replicated, may hold values from 0.5 to 1.5
- second_shift: float32 [410], replicated, may hold values from -2 to 2
- out_grad: bfloat16 [64, 256, 410], P('dp', 'tp'), may hold values from -6 to 6
Outputs:
- new_memory: bfloat16 [64, 256, 410], P('dp', 'tp')
- activations: bfloat16 [64, 256, 410], P('dp', 'tp')
- input_grad: float32 [64, 256, 410], P('dp', 'tp')
- grad_query: float32 [410, 410], replicated
- grad_key: float32 [410, 410], replicated
- grad_value: float32 [410, 410], replicated
- grad_pos: float32 [410, 410], replicated
- grad_bias_u: float32 [410], replicated
- grad_bias_v: float32 [410], replicated
- grad_out: float32 [410, 410], replicated
- grad_first_gain: float32 [410], replicated
- grad_first_shift: float32 [410], replicated
- grad_ffn_in: float32 [410, 2100], P(None, 'tp')
- grad_ffn_in_bias: float32 [2100], P('tp')
- grad_ffn_out: float32 [2100, 410], P('tp')
- grad_ffn_out_bias: float32 [410], replicated
- grad_second_gain: float32 [410], replicated
- grad_second_shift: float32 [410], replicated
Inputs may be any that keep to these rules, and one draw needn't show every extreme that they name: In each group of 4 consecutive streams one stream, which one drawn from the seed, has segment_length 256, memory_length 256 and no reset.
All inputs are finite; a program needn't handle non-finite values.
Results may differ from a plain program's by a relative error of at most 0.015.
Values may be sent and summed in bfloat16 or wider, within the bound.
No kernel may reach another device: no remote copies, remote signals or barrier semaphores. Data moves between devices by JAX's collectives and lax.ppermute only.
A program may use at most 192 MiB of HBM per device.

v0:
```python
import math

import jax
import jax.numpy as jnp
from jax import lax
from jax.sharding import PartitionSpec as P

D = 410
HEADS = 10
DHEAD = 41
SEG = 256
MEM = 256


EPSILON = 1e-05
NEG_LARGE = -1e30


def layer_norm(values, norm_gain, norm_shift):
    row_mean = jnp.mean(values, axis=-1, keepdims=True)
    centred = values - row_mean
    variance = jnp.mean(centred * centred, axis=-1, keepdims=True)
    return centred * lax.rsqrt(variance + EPSILON) * norm_gain + norm_shift


def position_table(feature_count, row_total, farthest):
    distance = farthest - jnp.arange(row_total).astype(jnp.float32)
    inverse = 1.0 / 10000.0 ** (jnp.arange(0, feature_count, 2).astype(jnp.float32) / feature_count)
    angles = distance[:, None] * inverse[None, :]
    return jnp.concatenate([jnp.sin(angles), jnp.cos(angles)], axis=1)


def heads_of(values):
    return values.reshape(values.shape[:-1] + (HEADS, DHEAD))


def smooth_gate(values):
    return jax.nn.gelu(values, approximate=True)


def shift_rows(full_rows, key_count):
    row_count = full_rows.shape[-2]
    span_rows = full_rows.shape[-1]
    leading = full_rows.shape[:-2]
    flat_rows = full_rows.reshape(leading + (row_count * span_rows,))
    flat_rows = flat_rows[..., row_count - 1 : row_count - 1 + row_count * (span_rows - 1)]
    return flat_rows.reshape(leading + (row_count, span_rows - 1))[..., :key_count]


def unshift_rows(grad_rows, span_rows):
    row_count = grad_rows.shape[-2]
    key_count = grad_rows.shape[-1]
    leading = grad_rows.shape[:-2]
    edges = [(0, 0)] * len(leading)
    padded = jnp.pad(grad_rows, edges + [(0, 0), (0, span_rows - 1 - key_count)])
    flat_rows = padded.reshape(leading + (row_count * (span_rows - 1),))
    flat_rows = jnp.pad(flat_rows, edges + [(row_count - 1, 1)])
    return flat_rows.reshape(leading + (row_count, span_rows))


def allowed_keys(doc_reset, segment_length, memory_length, first_row, row_count):
    documents = jnp.cumsum(doc_reset, axis=1)
    positions = jnp.arange(SEG)
    queries = first_row + jnp.arange(row_count)
    query_docs = lax.dynamic_slice_in_dim(documents, first_row, row_count, 1)
    slot_ids = jnp.arange(MEM)
    memory_ok = (slot_ids[None, None, :] >= (MEM - memory_length)[:, None, None]) & (
        query_docs[:, :, None] == 0
    )
    earlier = queries[None, :, None] > positions[None, None, :]
    same_doc = query_docs[:, :, None] == documents[:, None, :]
    is_valid = positions[None, None, :] < segment_length[:, None, None]
    diagonal = queries[None, :, None] == positions[None, None, :]
    return jnp.concatenate([memory_ok, earlier & same_doc & is_valid | diagonal], axis=2)


def block_scores(heads_u, heads_v, key_heads, rel_heads, allowed, factor):
    content = jnp.einsum("bqhe,bkhe->bhqk", heads_u, key_heads, preferred_element_type=jnp.float32)
    relative = jnp.einsum("bqhe,phe->bhqp", heads_v, rel_heads, preferred_element_type=jnp.float32)
    scores = (content + shift_rows(relative, key_heads.shape[1])) * factor
    return jnp.where(allowed[:, None], scores, NEG_LARGE)


def shards(
    hidden,
    memory,
    segment_length,
    memory_length,
    doc_reset,
    w_query,
    w_key,
    w_value,
    w_pos,
    bias_u,
    bias_v,
    w_out,
    first_gain,
    first_shift,
    ffn_in,
    ffn_in_bias,
    ffn_out,
    ffn_out_bias,
    second_gain,
    second_shift,
    out_grad,
):
    low_type = jnp.bfloat16
    wide_type = jnp.float32
    highest = lax.Precision.HIGHEST
    tp_index = lax.axis_index("tp")
    stream_count = hidden.shape[0]
    row_count = hidden.shape[1]
    mem_rows = memory.shape[1]
    key_count = MEM + SEG
    span_rows = key_count + row_count - 1
    first_row = tp_index * row_count
    table_start = SEG - first_row - row_count
    factor = 1.0 / math.sqrt(DHEAD)
    block_size = math.gcd(stream_count, max(1, 512 // row_count))
    block_count = stream_count // block_size

    def blocks_of(values):
        return values.reshape((block_count, block_size) + values.shape[1:])

    joined = jnp.concatenate([memory, hidden], axis=1)
    w_pair = jnp.concatenate([w_key, w_value], axis=1)
    w_pair_wide = w_pair.astype(wide_type)
    pair_local = jnp.einsum("nrd,df->nrf", joined, w_pair, preferred_element_type=wide_type).astype(
        low_type
    )
    pair_mem, pair_seg = (
        lax.all_gather(pair_local[:, :mem_rows], "tp", axis=1, tiled=True),
        lax.all_gather(pair_local[:, mem_rows:], "tp", axis=1, tiled=True),
    )
    pair_all = jnp.concatenate([pair_mem, pair_seg], axis=1)
    queries = jnp.einsum("nrd,df->nrf", hidden, w_query, preferred_element_type=wide_type)
    query_u = (queries + bias_u).astype(low_type)
    query_v = (queries + bias_v).astype(low_type)
    pos_table = position_table(D, span_rows, key_count - 1 - table_start).astype(low_type)
    rel_heads = heads_of(
        jnp.dot(pos_table, w_pos, preferred_element_type=wide_type).astype(low_type)
    )
    allowed = allowed_keys(doc_reset, segment_length, memory_length, first_row, row_count)

    def attend_block(packed):
        part_u, part_v, part_pair, part_allowed = packed
        scores = block_scores(
            heads_of(part_u),
            heads_of(part_v),
            heads_of(part_pair[..., :D]),
            rel_heads,
            part_allowed,
            factor,
        )
        top_score = jnp.max(scores, axis=-1, keepdims=True)
        exp_terms = jnp.exp(scores - top_score)
        row_total = jnp.sum(exp_terms, axis=-1, keepdims=True)
        probs_low = (exp_terms / row_total).astype(low_type)
        mixed_rows = jnp.einsum(
            "bhqk,bkhe->bqhe",
            probs_low,
            heads_of(part_pair[..., D:]),
            preferred_element_type=wide_type,
        )
        return (
            mixed_rows.reshape(mixed_rows.shape[:2] + (D,)).astype(low_type),
            top_score + jnp.log(row_total),
        )

    attended, log_totals = lax.map(
        attend_block,
        (blocks_of(query_u), blocks_of(query_v), blocks_of(pair_all), blocks_of(allowed)),
    )
    attended = attended.reshape(stream_count, row_count, D)
    branch = jnp.einsum("nrd,df->nrf", attended, w_out, preferred_element_type=wide_type)
    first_norm, first_back = jax.vjp(
        layer_norm, hidden.astype(wide_type) + branch, first_gain, first_shift
    )
    first_low = first_norm.astype(low_type)
    in_full, in_bias_full, out_full = (
        lax.all_gather(ffn_in, "tp", axis=1, tiled=True),
        lax.all_gather(ffn_in_bias, "tp", axis=0, tiled=True),
        lax.all_gather(ffn_out, "tp", axis=0, tiled=True),
    )
    inner_pre = jnp.einsum(
        "nrd,df->nrf", first_low, in_full, preferred_element_type=wide_type
    ) + in_bias_full.astype(wide_type)
    active, gate_back = jax.vjp(smooth_gate, inner_pre)
    active_low = active.astype(low_type)
    ffn_part = jnp.einsum("nrf,fd->nrd", active_low, out_full, preferred_element_type=wide_type)
    second_out, second_back = jax.vjp(
        layer_norm, first_norm + ffn_part + ffn_out_bias, second_gain, second_shift
    )
    grad_second, grad_second_gain, grad_second_shift = second_back(out_grad.astype(wide_type))
    grad_out_bias = jnp.sum(grad_second, axis=(0, 1))
    grad_second_low = grad_second.astype(low_type)
    grad_active = jnp.einsum(
        "nrd,fd->nrf", grad_second_low, out_full, preferred_element_type=wide_type
    )
    grad_inner = gate_back(grad_active)[0].astype(low_type)
    grad_ffn_out = jnp.einsum(
        "nrf,nrd->fd", active_low, grad_second_low, preferred_element_type=wide_type
    )
    grad_ffn_in = jnp.einsum("nrd,nrf->df", first_low, grad_inner, preferred_element_type=wide_type)
    grad_ffn_in_bias = jnp.sum(grad_inner, axis=(0, 1), dtype=wide_type)
    grad_first_part = jnp.einsum(
        "nrf,df->nrd", grad_inner, in_full, preferred_element_type=wide_type
    )
    ffn_grads = (
        lax.psum_scatter(
            grad_ffn_in.astype(jnp.bfloat16), "tp", scatter_dimension=1, tiled=True
        ).astype(jnp.float32),
        lax.psum_scatter(
            grad_ffn_in_bias.astype(jnp.bfloat16), "tp", scatter_dimension=0, tiled=True
        ).astype(jnp.float32),
        lax.psum_scatter(
            grad_ffn_out.astype(jnp.bfloat16), "tp", scatter_dimension=0, tiled=True
        ).astype(jnp.float32),
    )
    grad_first_pre, grad_first_gain, grad_first_shift = first_back(grad_second + grad_first_part)
    grad_branch = grad_first_pre.astype(low_type)
    grad_out_w = jnp.einsum("nrd,nrf->df", attended, grad_branch, preferred_element_type=wide_type)
    grad_attended = jnp.einsum(
        "nrf,df->nrd", grad_branch, w_out, preferred_element_type=wide_type
    ).astype(low_type)

    def attend_back(rel_grad, packed):
        part_u, part_v, part_pair, part_allowed, part_log, part_grad = packed
        heads_u = heads_of(part_u)
        heads_v = heads_of(part_v)
        key_heads = heads_of(part_pair[..., :D])
        value_heads = heads_of(part_pair[..., D:])
        scores = block_scores(heads_u, heads_v, key_heads, rel_heads, part_allowed, factor)
        attn_probs = jnp.exp(scores - part_log)
        grad_heads = heads_of(part_grad)
        grad_values = jnp.einsum(
            "bhqk,bqhe->bkhe",
            attn_probs.astype(low_type),
            grad_heads,
            preferred_element_type=wide_type,
        )
        grad_probs = jnp.einsum(
            "bqhe,bkhe->bhqk", grad_heads, value_heads, preferred_element_type=wide_type
        )
        row_inner = jnp.sum(grad_probs * attn_probs, axis=-1, keepdims=True)
        grad_scores = (attn_probs * (grad_probs - row_inner)).astype(low_type)
        grad_u = (
            jnp.einsum("bhqk,bkhe->bqhe", grad_scores, key_heads, preferred_element_type=wide_type)
            * factor
        )
        grad_keys = (
            jnp.einsum("bhqk,bqhe->bkhe", grad_scores, heads_u, preferred_element_type=wide_type)
            * factor
        )
        grad_rel = unshift_rows(grad_scores, span_rows)
        grad_v = (
            jnp.einsum("bhqp,phe->bqhe", grad_rel, rel_heads, preferred_element_type=wide_type)
            * factor
        )
        rel_grad = (
            rel_grad
            + jnp.einsum("bhqp,bqhe->phe", grad_rel, heads_v, preferred_element_type=wide_type)
            * factor
        )
        flat_shape = grad_u.shape[:2] + (D,)
        pair_shape = grad_keys.shape[:2] + (D,)
        pair_grad = jnp.concatenate(
            [grad_keys.reshape(pair_shape), grad_values.reshape(pair_shape)], axis=-1
        )
        return (rel_grad, (grad_u.reshape(flat_shape), grad_v.reshape(flat_shape), pair_grad))

    rel_grad, (grad_u_all, grad_v_all, grad_pair) = lax.scan(
        attend_back,
        jnp.zeros((span_rows, HEADS, DHEAD), wide_type),
        (
            blocks_of(query_u),
            blocks_of(query_v),
            blocks_of(pair_all),
            blocks_of(allowed),
            log_totals,
            blocks_of(grad_attended),
        ),
    )
    grad_u_all = grad_u_all.reshape(stream_count, row_count, D)
    grad_v_all = grad_v_all.reshape(stream_count, row_count, D)
    grad_pair = grad_pair.reshape(stream_count, key_count, 2 * D)
    own_mem, own_seg = (
        lax.psum_scatter(
            grad_pair[:, :MEM].astype(jnp.bfloat16), "tp", scatter_dimension=1, tiled=True
        ).astype(jnp.float32),
        lax.psum_scatter(
            grad_pair[:, MEM:].astype(jnp.bfloat16), "tp", scatter_dimension=1, tiled=True
        ).astype(jnp.float32),
    )
    own_pair = jnp.concatenate([own_mem, own_seg], axis=1)
    grad_pair_w = jnp.einsum(
        "nrd,nrf->df",
        joined.astype(wide_type),
        own_pair,
        precision=highest,
        preferred_element_type=wide_type,
    )
    key_input = jnp.einsum(
        "nrf,df->nrd", own_seg, w_pair_wide, precision=highest, preferred_element_type=wide_type
    )
    grad_queries = (grad_u_all + grad_v_all).astype(low_type)
    grad_query_w = jnp.einsum("nrd,nrf->df", hidden, grad_queries, preferred_element_type=wide_type)
    input_grad = (
        grad_first_pre
        + jnp.einsum("nrf,df->nrd", grad_queries, w_query, preferred_element_type=wide_type)
        + key_input
    )
    grad_pos_w = jnp.einsum(
        "pd,pf->df",
        pos_table.astype(wide_type),
        rel_grad.reshape(span_rows, D),
        precision=highest,
        preferred_element_type=wide_type,
    )
    summed = lax.psum(
        (
            grad_query_w,
            grad_pair_w,
            grad_pos_w,
            grad_out_w,
            jnp.sum(grad_u_all, axis=(0, 1)),
            jnp.sum(grad_v_all, axis=(0, 1)),
            grad_first_gain,
            grad_first_shift,
            grad_second_gain,
            grad_second_shift,
            grad_out_bias,
        ),
        ("dp", "tp"),
    )
    ffn_grads = lax.psum((ffn_grads[0], ffn_grads[1], ffn_grads[2]), "dp")
    documents = jnp.cumsum(doc_reset, axis=1)
    own_docs = lax.dynamic_slice_in_dim(documents, first_row, row_count, 1)
    own_positions = first_row + jnp.arange(row_count)
    keep_rows = (own_docs == documents[:, -1:]) & (own_positions[None, :] < segment_length[:, None])
    new_memory = jnp.where(keep_rows[:, :, None], hidden, jnp.zeros_like(hidden))
    return (
        new_memory,
        second_out.astype(low_type),
        input_grad,
        summed[0],
        summed[1][:, :D],
        summed[1][:, D:],
        summed[2],
        summed[4],
        summed[5],
        summed[3],
        summed[6],
        summed[7],
        ffn_grads[0],
        ffn_grads[1],
        ffn_grads[2],
        summed[10],
        summed[8],
        summed[9],
    )


def solution(mesh):
    placed = (
        P("dp", "tp", None),
        P("dp", "tp", None),
        P("dp"),
        P("dp"),
        P("dp", None),
        P(),
        P(),
        P(),
        P(),
        P(),
        P(),
        P(),
        P(),
        P(),
        P(None, "tp"),
        P("tp"),
        P("tp", None),
        P(),
        P(),
        P(),
        P("dp", "tp", None),
    )
    return jax.shard_map(
        shards,
        mesh=mesh,
        in_specs=placed,
        out_specs=(
            P("dp", "tp", None),
            P("dp", "tp", None),
            P("dp", "tp", None),
            P(),
            P(),
            P(),
            P(),
            P(),
            P(),
            P(),
            P(),
            P(),
            P(None, "tp"),
            P("tp"),
            P("tp", None),
            P(),
            P(),
            P(),
        ),
        check_vma=False,
    )
```

profile of v0, /device:TPU:0, one launch (start us, length us, event | category | flops | bytes accessed | tf_op | source)
XLA Modules:
  0.0 614.0 jit_solution(2340257535543142816)
XLA Ops:
  9.5 2.7 convolution_convert_fusion
  12.3 1.5 fusion.97
  19.4 2.6 all-reduce.2
  22.1 2.7 fusion.62
  29.1 6.7 %convolution_bitcast_fusion = f32[4,10,128,639]{2,3,0,1:T(8,128)} fusion(bf16[639,10,41,1]{0,2,1,3:T(8,128)(2,1)S(1)} %reshape.386, bf16[4,128,10,41]{1,0,3,2:T(4,128)(2,1)S(1)} %bitcast.141), kind=kOutput, calls=%fused_computation.9 | convolution fusion | flops 268277760 | bytes 14030540 | tf_op jit(solution)/shard_map/while/body/eval_jaxpr/bqhe,phe->bhqp/dot_general | solution.py:79
  35.8 14.2 %copy.119 = f32[4,10,128,639]{3,2,0,1:T(8,128)} copy(f32[4,10,128,639]{2,3,0,1:T(8,128)} %convolution_bitcast_fusion) | data formatting | bytes 26173440 | tf_op jit(solution)/shard_map/while/body/eval_jaxpr/bqhe,phe->bhqp/transpose | solution.py:79
  50.0 18.6 %reshape.367 = f32[4,10,81792]{2,0,1:T(4,128)} reshape(f32[4,10,128,639]{3,2,0,1:T(8,128)} %copy.119) | data formatting | bytes 26173440 | tf_op jit(solution)/shard_map/while/body/eval_jaxpr/reshape | solution.py:45
  68.6 13.8 %slice.72 = f32[4,10,81664]{2,0,1:T(4,128)} slice(f32[4,10,81792]{2,0,1:T(4,128)} %reshape.367), slice={[0:4], [0:10], [127:81791]} | slice | bytes 26132480 | tf_op jit(solution)/shard_map/while/body/eval_jaxpr/slice | solution.py:46
  82.4 20.1 %reshape.368 = f32[4,10,128,638]{3,2,0,1:T(8,128)} reshape(f32[4,10,81664]{2,0,1:T(4,128)} %slice.72) | data formatting | bytes 26132480 | tf_op jit(solution)/shard_map/while/body/eval_jaxpr/reshape | solution.py:47
  103.5 2.8 constant_dynamic-update-slice_fusion.1
  106.3 2.8 constant_dynamic-update-slice_fusion
  109.1 2.6 fusion.95
  111.7 2.5 copy.110
  115.5 4.9 fusion.101
  120.5 2.4 fusion.2
  122.8 1.7 copy-done.1
  124.6 3.3 fusion.54
  129.7 4.2 copy.125
  133.9 5.1 reshape.388
  139.1 4.2 copy.126
  143.3 4.9 reshape.389
  148.3 3.5 convolution_add_fusion
  151.8 1.9 fusion.103
  155.6 4.7 fusion.104
  160.4 1.5 multiply_reduce_fusion.1
  163.7 3.6 fusion.19
  167.3 4.2 multiply_reduce_fusion
  171.4 2.9 copy.139
  174.3 2.4 multiply_convert_fusion
  177.6 1.4 copy-done.2
  180.4 2.2 maximum_convert_fusion
  182.5 2.9 fusion.96
  185.4 4.5 copy.159
  189.9 2.2 reshape.403
  192.2 4.5 copy.157
  196.6 2.2 reshape.401
  199.1 4.4 fusion.17
  203.6 5.4 fusion.18
  209.0 3.1 copy.169
  212.1 3.6 pad.10.clone
  215.7 13.8 %reshape.370 = bf16[4,10,81664]{2,0,1:T(4,128)(2,1)} reshape(bf16[4,10,128,638]{3,2,0,1:T(8,128)(2,1)} %pad.10.clone) | data formatting | bytes 13066240 | tf_op jit(solution)/shard_map/while/body/eval_jaxpr/reshape | solution.py:56
  229.5 10.3 %pad.11 = bf16[4,10,81792]{2,0,1:T(4,128)(2,1)} pad(bf16[4,10,81664]{2,0,1:T(4,128)(2,1)} %reshape.370, bf16[]{:T(256)} %constant.61.clone.1), padding=0_0x0_0x127_1 | pad | bytes 13076482 | tf_op jit(solution)/shard_map/while/body/eval_jaxpr/jit(_pad)/pad | solution.py:57
  239.8 17.0 %reshape.371 = bf16[4,10,128,639]{3,2,0,1:T(8,128)(2,1)} reshape(bf16[4,10,81792]{2,0,1:T(4,128)(2,1)} %pad.11) | data formatting | bytes 13086720 | tf_op jit(solution)/shard_map/while/body/eval_jaxpr/reshape | solution.py:58
  256.9 5.0 fusion.36
  261.8 2.6 reshape.374
  264.5 5.1 fusion.40
  269.6 2.2 fusion.99
  274.7 2.6 fusion.77
  277.3 2.5 reshape.404
  279.8 1.7 copy.160
  281.5 2.5 reshape.402
  285.3 4.0 fusion.32
  290.2 2.8 dynamic-slice_convert_fusion.1
  293.1 2.9 dynamic-slice_convert_fusion
  297.2 2.0 copy.146
  299.5 42.8 %all-reduce.6 = (f32[410]{0:T(512)}, f32[410]{0:T(512)}, f32[410]{0:T(512)}, f32[410]{0:T(512)}, f32[410]{0:T(512)}, /*index=5*/f32[410]{0:T(512)}, f32[410]{0:T(512)}) all-reduce(f32[410]{0:T(512)S(1)} %reduce_sum.214, f32[410]{0:T(512)S(1)} %reduce_sum.216, ...), channel_id=1, replica_groups=mesh['dp'=16,'tp'=2] {'dp','tp'}, use_global_device_ids=true, to_apply=%region_19.20 | all-reduce | flops 2870 | bytes 22960 | tf_op jit(solution)/shard_map/psum | solution.py:320
  342.4 2.5 all-reduce.4
  344.9 42.6 %psum.107 = f32[1050]{0:T(1024)} all-reduce(f32[1050]{0:T(1024)S(1)} %dynamic-slice_convert_fusion.2), channel_id=1, replica_groups=mesh['dp'=16,'tp'=2] {'dp'}, use_global_device_ids=true, to_apply=%region_31.32 | all-reduce | flops 1050 | bytes 8400 | tf_op jit(solution)/shard_map/psum | solution.py:336
  387.6 2.0 fusion.71
  390.0 1.4 copy.147
  391.5 43.9 %all-reduce.14.cloned.1.call-done = (f32[410,410]{0,1:T(8,128)}, f32[410,820]{1,0:T(8,128)}, f32[410,410]{1,0:T(8,128)}, f32[410,410]{1,0:T(8,128)}) async-done(((f32[410,410]{0,1:T(8,128)}, f32[410,820]{1,0:T(8,128)}, f32[410,410]{1,0:T(8,128)}, f32[410,410]{1,0:T(8,128)}), (f32[410,410]{0,1:T(8,128)}, f32[410,820]{1,0:T(8,128)}, f32[410,410]{1,0:T(8,128)}, ...) | async-done | bytes 3362016 | tf_op jit(solution)/shard_map/psum | solution.py:320
  435.3 2.5 copy.148
  437.8 2.9 fusion.98
  440.7 161.9 %all-reduce.16.cloned.1.call-done = (f32[410,1050]{1,0:T(8,128)}, f32[1050,410]{0,1:T(8,128)}) async-done(((f32[410,1050]{1,0:T(8,128)}, f32[1050,410]{0,1:T(8,128)}), (f32[410,1050]{1,0:T(8,128)}, f32[1050,410]{0,1:T(8,128)})) %all-reduce.16.cloned.1.call-update) | async-done | bytes 3444016 | tf_op jit(solution)/shard_map/psum | solution.py:336
  (217 shorter events, 32.4 us)
Async XLA Ops:
  7.2 19.4 %copy-start = (bf16[410,410]{1,0:T(8,128)(2,1)S(1)}, bf16[410,410]{1,0:T(8,128)(2,1)}, u32[]{:S(2)}) copy-start(bf16[410,410]{1,0:T(8,128)(2,1)} %param.26) | copy-start | bytes 1008604
  7.2 96.3 %all-gather.7.cloned.1.call-start = ((), (), s32[]{:S(2)}) async-start(), calls=%async_computation.2 | async-start | bytes 2531328 | tf_op jit(solution)/shard_map/all_gather | solution.py:132
  9.5 4.3 copy-start.38
  12.2 3.8 copy-start.54
  12.3 3.9 copy-start.47
  12.3 3.9 copy-start.40
  12.3 5.6 copy-start.44
  12.3 6.8 %copy-start.41 = (bf16[1050]{0:T(1024)(128)(2,1)S(1)}, bf16[1050]{0:T(1024)(128)(2,1)}, u32[]{:S(2)}) copy-start(bf16[1050]{0:T(1024)(128)(2,1)} %param.36) | copy-start | bytes 6304
  12.3 13.4 %copy-start.49 = (bf16[410,410]{1,0:T(8,128)(2,1)S(1)}, bf16[410,410]{1,0:T(8,128)(2,1)}, u32[]{:S(2)}) copy-start(bf16[410,410]{1,0:T(8,128)(2,1)} %param.29) | copy-start | bytes 1008604
  13.8 12.8 %copy-start.13 = (bf16[4,128,410]{1,0,2:T(4,128)(2,1)S(1)}, bf16[4,128,410]{1,0,2:T(4,128)(2,1)}, u32[]{:S(2)}) copy-start(bf16[4,128,410]{1,0,2:T(4,128)(2,1)} %param.21) | copy-start | bytes 1259524
  13.8 12.8 %copy-start.50 = (f32[410]{0:T(512)S(1)}, f32[410]{0:T(512)}, u32[]{:S(2)}) copy-start(f32[410]{0:T(512)} %param.30) | copy-start | bytes 4924
  13.8 12.8 %copy-start.51 = (f32[410]{0:T(512)S(1)}, f32[410]{0:T(512)}, u32[]{:S(2)}) copy-start(f32[410]{0:T(512)} %param.31) | copy-start | bytes 4924
  13.9 92.4 %all-gather.9.cloned.1.call-start = ((), (), s32[]{:S(2)}) async-start(), calls=%async_computation.3 | async-start | bytes 2531328 | tf_op jit(solution)/shard_map/all_gather | solution.py:133
  14.6 115.1 %all-gather.11.cloned.1.call-start = ((), (), s32[]{:S(2)}) async-start(), calls=%async_computation.4 | async-start | bytes 2875392 | tf_op jit(solution)/shard_map/all_gather | solution.py:181
  15.3 123.7 %all-gather.13.cloned.1.call-start = ((), (), s32[]{:S(2)}) async-start(), calls=%async_computation.5 | async-start | bytes 2875392 | tf_op jit(solution)/shard_map/all_gather | solution.py:183
  15.9 261.3 %reduce-scatter.11.cloned.1.call-start = ((), (), s32[]{:S(2)}) async-start(), calls=%async_computation.7 | async-start | bytes 2555904
  16.0 12.3 %copy-start.42 = (s32[128]{0:T(128)}, s32[128]{0:T(128)S(1)}, u32[]{:S(2)}) copy-start(s32[128]{0:T(128)S(1)} %iota_add_fusion) | copy-start | bytes 1540
  26.6 9.1 %copy-start.20 = (bf16[639,10,41,1]{0,2,1,3:T(8,128)(2,1)}, bf16[639,10,41,1]{0,2,1,3:T(8,128)(2,1)S(1)}, u32[]{:S(2)}) copy-start(bf16[639,10,41,1]{0,2,1,3:T(8,128)(2,1)S(1)} %reshape.386) | copy-start | bytes 1571944
  109.1 6.4 %copy-start.3 = (f32[4,10,128,638]{3,2,0,1:T(8,128)S(1)}, f32[4,10,128,638]{3,2,0,1:T(8,128)}, u32[]{:S(2)}) copy-start(f32[4,10,128,638]{3,2,0,1:T(8,128)} %reshape.368) | copy-start | bytes 39198724
  115.5 5.0 copy-start.4
  120.5 4.1 copy-start.1
  120.5 4.1 copy-start.8
  124.6 3.6 copy-start.14
  124.6 3.6 copy-start.36
  128.1 10.9 %copy-start.26 = (bf16[4,128,10,41]{1,0,3,2:T(4,128)(2,1)}, bf16[4,128,10,41]{1,0,3,2:T(4,128)(2,1)S(1)}, u32[]{:S(2)}) copy-start(bf16[4,128,10,41]{1,0,3,2:T(4,128)(2,1)S(1)} %copy.122) | copy-start | bytes 1259524
  139.0 9.2 %copy-start.46 = (f32[410]{0:T(512)S(1)}, f32[410]{0:T(512)}, u32[]{:S(2)}) copy-start(f32[410]{0:T(512)} %param.33) | copy-start | bytes 4924
  139.0 9.2 %copy-start.53 = (f32[410]{0:T(512)S(1)}, f32[410]{0:T(512)}, u32[]{:S(2)}) copy-start(f32[410]{0:T(512)} %param.34) | copy-start | bytes 4924
  148.2 3.5 copy-start.19
  148.2 3.5 copy-start.25
  148.2 3.5 copy-start.52
  151.8 3.8 copy-start.56
  151.8 2.0 copy-start.28
  151.8 2.0 copy-start.39
  151.8 2.4 copy-start.45
  155.5 4.8 copy-start.15
  155.6 8.1 %slice-start = ((s8[10485760]{0:T(1024)(128)(4,1)}), s8[4194304]{0:T(1024)(128)(4,1)S(1)}, s32[]{:S(2)}) async-start(s8[10485760]{0:T(1024)(128)(4,1)} %bitcast.127), calls=%async_computation.11 | async-start | bytes 8388608
  155.6 4.8 copy-start.24
  155.6 8.1 %slice-start.1 = ((s8[10485760]{0:T(1024)(128)(4,1)}), s8[4194304]{0:T(1024)(128)(4,1)S(1)}, s32[]{:S(2)}) async-start(s8[10485760]{0:T(1024)(128)(4,1)} %bitcast.127), calls=%async_computation.12 | async-start | bytes 8388608
  155.6 8.1 %slice-start.2 = ((s8[10485760]{0:T(1024)(128)(4,1)}), s8[2097152]{0:T(1024)(128)(4,1)S(1)}, s32[]{:S(2)}) async-start(s8[10485760]{0:T(1024)(128)(4,1)} %bitcast.127), calls=%async_computation.13 | async-start | bytes 4194304
  160.3 2.7 copy-start.37
  174.3 2.4 copy-start.11
  176.8 2.3 copy-start.2
  192.1 89.4 %reduce-scatter.9.cloned.1.call-start = ((), (), s32[]{:S(2)}) async-start(), calls=%async_computation.6 | async-start | bytes 2555904
  198.9 4.7 copy-start.16
  198.9 91.3 %all-reduce.18.cloned.1.call-start = ((), (), s32[]{:S(2)}) async-start(), calls=%async_computation.10 | async-start | bytes 7241728
  208.9 226.4 %all-reduce.14.cloned.1.call-start = ((), (), s32[]{:S(2)}) async-start(), calls=%async_computation.8 | async-start | bytes 8093696 | tf_op jit(solution)/shard_map/psum | solution.py:320
  239.8 17.0 %copy-start.10 = (bf16[4,128,410]{1,0,2:T(4,128)(2,1)S(1)}, bf16[4,128,410]{1,0,2:T(4,128)(2,1)}, u32[]{:S(2)}) copy-start(bf16[4,128,410]{1,0,2:T(4,128)(2,1)} %copy-done.9) | copy-start | bytes 1259524
  261.8 7.7 %slice-start.3 = ((s8[6553600]{0:T(1024)(128)(4,1)}), s8[2359296]{0:T(1024)(128)(4,1)S(1)}, s32[]{:S(2)}) async-start(s8[6553600]{0:T(1024)(128)(4,1)} %bitcast.129), calls=%async_computation.14 | async-start | bytes 4718592
  264.5 5.1 slice-start.4
  264.5 5.1 copy-start.21
  269.6 3.8 copy-start.6
  269.6 3.8 copy-start.27
  271.8 2.9 copy-start.12
  271.8 2.9 copy-start.30
  271.8 2.9 copy-start.32
  285.2 4.0 copy-start.35
  289.2 313.4 %all-reduce.16.cloned.1.call-start = ((), (), s32[]{:S(2)}) async-start(), calls=%async_computation.9 | async-start | bytes 7667712 | tf_op jit(solution)/shard_map/psum | solution.py:336
  293.1 3.1 copy-start.43
  293.1 3.1 copy-start.48
  293.1 6.3 %copy-start.17 = (f32[4,128,410]{1,2,0:T(8,128)S(1)}, f32[4,128,410]{1,2,0:T(8,128)}, u32[]{:S(2)}) copy-start(f32[4,128,410]{1,2,0:T(8,128)} %copy-done.15) | copy-start | bytes 2519044
  296.0 93.6 %copy-start.7 = (f32[4,128,410]{1,2,0:T(8,128)S(1)}, f32[4,128,410]{1,2,0:T(8,128)}, u32[]{:S(2)}) copy-start(f32[4,128,410]{1,2,0:T(8,128)} %copy-done.5) | copy-start | bytes 2519044
  435.3 167.3 %copy-start.34 = (f32[410,410]{1,0:T(8,128)S(1)}, f32[410,410]{1,0:T(8,128)}, u32[]{:S(2)}) copy-start(f32[410,410]{1,0:T(8,128)} %get-tuple-element.198) | copy-start | bytes 2017204
  435.3 168.2 %copy-start.33 = (f32[410,410]{1,0:T(8,128)S(1)}, f32[410,410]{1,0:T(8,128)}, u32[]{:S(2)}) copy-start(f32[410,410]{1,0:T(8,128)} %get-tuple-element.201) | copy-start | bytes 2017204
  602.6 3.1 copy-start.22
  (7 other events, 7.5 us)
Sparse Core Ops, SparseCore 0:
  13.9 12.4 all-gather.6
  28.6 10.9 all-gather.8
  41.2 11.4 all-gather.10
  54.1 11.4 all-gather.12
  192.2 11.9 reduce-scatter.10
  206.4 10.3 reduce-scatter.8
  219.8 25.3 all-reduce.17
  289.4 145.9 all-reduce.13
  441.8 160.8 all-reduce.15
where the time goes:
time: 625 us; the launch traced here: 614 us
  waiting for transfers between devices  208 us (33%)
  local copies, waits for them, and re-layouts  203 us (32%)
  blocking collectives  90.5 us (14%)
  matrix products  73.4 us (12%)
  other arithmetic  21.5 us (3%)
  between operations  16.7 us (3%)
    psum x1, waiting for transfers between devices, shards(): ffn_grads = lax.psum((ffn_grads[0], ffn_grads[1], ffn_grads[2]), 'dp')  162 us
    unnamed x149, local copies, waits for them, and re-layouts  56.4 us
    psum x1, waiting for transfers between devices, shards(): lax.psum((grad_query_w, grad_pair_w, grad_pos_w, grad_out_w, jnp.sum(grad...  43.9 us
    psum x1, blocking collectives, shards(): lax.psum((grad_query_w, grad_pair_w, grad_pos_w, grad_out_w, jnp.sum(grad...  42.8 us
    psum x1, blocking collectives, shards(): ffn_grads = lax.psum((ffn_grads[0], ffn_grads[1], ffn_grads[2]), 'dp')  42.6 us
    reshape x1, local copies, waits for them, and re-layouts, shift_rows(): flat_rows.reshape(leading + (row_count, span_rows - 1))[..., :key_count]  20.1 us
    reshape x1, local copies, waits for them, and re-layouts, shift_rows(): flat_rows = full_rows.reshape(leading + (row_count * span_rows,))  18.6 us
    reshape x1, local copies, waits for them, and re-layouts, unshift_rows(): return flat_rows.reshape(leading + (row_count, span_rows))  17 us
  transfers between devices with their start and end apart: 9, of which 2 were waited for; matrix products, arithmetic and copies ran while one was open for 38% of the time, Pallas kernels for 0%

commit v1 on v0

v1 whole, which is shorter than its diff:
```python
import math

import jax
import jax.numpy as jnp
import ml_dtypes
import numpy as np
from jax import lax
from jax.experimental import pallas as pl
from jax.experimental.pallas import tpu as pltpu
from jax.sharding import PartitionSpec as P

D = 410
HEADS = 10
DHEAD = 41
SEG = 256
MEM = 256
KEYS = MEM + SEG
HALF = 128
PAIRS = HEADS // 2
WIDE = PAIRS * 128
ROWS = 416
SPAN = 768
EPSILON = 1e-05
NEG_LARGE = -1e30
FACTOR = 1.0 / math.sqrt(DHEAD)
LOW = jnp.bfloat16
F32 = jnp.float32
VMEM_BYTES = 56 * 1024 * 1024


def position_table():
    distance = (KEYS - 1 - np.arange(SPAN)).astype(np.float32)
    inverse = np.float32(1.0) / np.float32(10000.0) ** (
        np.arange(0, D, 2).astype(np.float32) / np.float32(D)
    )
    angles = distance[:, None] * inverse[None, :].astype(np.float32)
    table = np.concatenate([np.sin(angles), np.cos(angles)], axis=1)
    return table.astype(ml_dtypes.bfloat16)


def mm(left, right):
    return lax.dot_general(left, right, (((1,), (0,)), ((), ())), preferred_element_type=F32)


def mm_nt(left, right):
    return lax.dot_general(left, right, (((1,), (1,)), ((), ())), preferred_element_type=F32)


def expander(rows):
    row = lax.broadcasted_iota(jnp.int32, (rows, WIDE), 0)
    lane = lax.broadcasted_iota(jnp.int32, (rows, WIDE), 1)
    inside = lane & 63
    hit = (inside < DHEAD) & (row == (lane >> 6) * DHEAD + inside)
    return jnp.where(hit, 1.0, 0.0).astype(LOW)


def compressor():
    row = lax.broadcasted_iota(jnp.int32, (WIDE, D), 0)
    lane = lax.broadcasted_iota(jnp.int32, (WIDE, D), 1)
    inside = row & 63
    hit = (inside < DHEAD) & (lane == (row >> 6) * DHEAD + inside)
    return jnp.where(hit, 1.0, 0.0).astype(LOW)


def identity(size):
    row = lax.broadcasted_iota(jnp.int32, (size, size), 0)
    lane = lax.broadcasted_iota(jnp.int32, (size, size), 1)
    return jnp.where(row == lane, 1.0, 0.0).astype(LOW)


def reversal(size):
    row = lax.broadcasted_iota(jnp.int32, (size, size), 0)
    lane = lax.broadcasted_iota(jnp.int32, (size, size), 1)
    return jnp.where(row + lane == size - 1, 1.0, 0.0).astype(LOW)


def prep_kernel(wq, wk, wv, wp, wo, bias_u, bias_v, pos, o_q, o_kv, o_rel, o_wo, o_bias):
    expand = expander(D)
    q_wide = mm(wq[...], expand).astype(LOW)
    k_wide = mm(wk[...], expand).astype(LOW)
    v_wide = mm(wv[...], expand).astype(LOW)
    rel = mm(pos[...], wp[...]).astype(LOW)
    rel = mm(rel, expand).astype(LOW)
    for bias_index, bias in enumerate((bias_u, bias_v)):
        value = jnp.broadcast_to(bias[...], (8, D))
        high = value.astype(LOW)
        rest = value - high.astype(F32)
        middle = rest.astype(LOW)
        last = (rest - middle.astype(F32)).astype(LOW)
        wide = mm(high, expand) + mm(middle, expand) + mm(last, expand)
        for p in range(PAIRS):
            o_bias[p, bias_index] = wide[:, 128 * p : 128 * p + 128]
    for p in range(PAIRS):
        part = slice(128 * p, 128 * p + 128)
        o_q[p] = q_wide[:, part]
        o_kv[p, :, :128] = k_wide[:, part]
        o_kv[p, :, 128:] = v_wide[:, part]
        o_rel[p] = rel[:, part]
    o_wo[...] = mm(compressor(), wo[...]).astype(LOW)


def attend_kernel(
    place, seg_len, mem_len, hidden, memory, received, reset, wq, wkv, rel, bias,
    o_probs, o_kv, o_uv, o_att, o_joined, mask
):
    core = place[0]
    stream = pl.program_id(0)
    own = 2 * core + stream
    mine = pl.multiple_of(HALF * core, HALF)
    other = pl.multiple_of(HALF * (1 - core), HALF)

    @pl.when(pl.program_id(1) == 0)
    def start():
        o_joined[0, pl.ds(mine, HALF)] = memory[own]
        o_joined[0, pl.ds(other, HALF)] = received[2 + stream]
        o_joined[0, pl.ds(MEM + mine, HALF)] = hidden[own]
        o_joined[0, pl.ds(MEM + other, HALF)] = received[stream]
        starts = jnp.broadcast_to(reset[pl.ds(own, 1), :].astype(F32), (8, SEG)).astype(LOW)
        row = lax.broadcasted_iota(jnp.int32, (SEG, SEG), 0)
        lane = lax.broadcasted_iota(jnp.int32, (SEG, SEG), 1)
        lower = jnp.where(row >= lane, 1.0, 0.0).astype(LOW)
        doc_column = mm_nt(lower, starts)[:, :1]
        doc_row = mm_nt(starts, lower)[:1, :]
        memory_ok = (lane >= MEM - mem_len[own]) & (doc_column == 0.0)
        segment_ok = ((row > lane) & (doc_row == doc_column) & (lane < seg_len[own])) | (row == lane)
        mask[:, :MEM] = jnp.where(memory_ok, 0.0, NEG_LARGE)
        mask[:, MEM:] = jnp.where(segment_ok, 0.0, NEG_LARGE)

    pair_rows = mm(o_joined[0], wkv[0]).astype(LOW)
    o_kv[0, 0] = pair_rows
    queries = mm(o_joined[0, MEM:], wq[0])
    query_u = (queries + bias[0, 0, :1]).astype(LOW)
    query_v = (queries + bias[0, 1, :1]).astype(LOW)
    o_uv[0, 0, :, :128] = query_u
    o_uv[0, 0, :, 128:] = query_v
    first_head = lax.broadcasted_iota(jnp.int32, (HALF, 128), 1) < 64
    zero = jnp.zeros((HALF, 128), LOW)
    for b in range(2):
        count = KEYS if b else KEYS - HALF
        width = count + HALF
        rows = slice(HALF * b, HALF * b + HALF)
        start_row = HALF - HALF * b
        outs = []
        for h in range(2):
            if h == 0:
                u_h = jnp.where(first_head, query_u[rows], zero)
                v_h = jnp.where(first_head, query_v[rows], zero)
            else:
                u_h = jnp.where(first_head, zero, query_u[rows])
                v_h = jnp.where(first_head, zero, query_v[rows])
            content = mm_nt(u_h, pair_rows[:count, :128])
            relative = mm_nt(v_h, rel[0, start_row : start_row + width])
            relative = pltpu.roll(relative, count + 1, 1, stride=1, stride_axis=0)[:, :count]
            scores = (content + relative) * FACTOR + mask[rows, :count]
            exp_terms = jnp.exp(scores - jnp.max(scores, axis=1, keepdims=True))
            total = jnp.sum(exp_terms, axis=1, keepdims=True)
            probs = (exp_terms * (1.0 / total)).astype(LOW)
            o_probs[0, 0, h, rows, :count] = probs
            if b == 0:
                o_probs[0, 0, h, rows, count:] = jnp.zeros((HALF, HALF), LOW)
            outs.append(mm(probs, pair_rows[:count, 128:]))
        o_att[0, rows] = jnp.where(first_head, outs[0], outs[1]).astype(LOW)


def norm_forward(values):
    centred = values - jnp.mean(values, axis=1, keepdims=True)
    scale = lax.rsqrt(jnp.mean(centred * centred, axis=1, keepdims=True) + EPSILON)
    return centred * scale, scale


def norm_backward(grad, x_hat, scale):
    return scale * (
        grad
        - jnp.mean(grad, axis=1, keepdims=True)
        - x_hat * jnp.mean(grad * x_hat, axis=1, keepdims=True)
    )


GELU_A = math.sqrt(2.0 / math.pi)
GELU_B = 0.044715


def gelu_both(x):
    square = x * x
    bent = jnp.tanh(x * (GELU_A + (GELU_A * GELU_B) * square))
    half_up = 0.5 + 0.5 * bent
    slope = half_up + (0.5 * x) * (1.0 - bent * bent) * (GELU_A + (3.0 * GELU_A * GELU_B) * square)
    return x * half_up, slope


def total_rows(values):
    return jnp.sum(values, axis=0, keepdims=True)


def ffn_kernel(
    place, att, joined, out_grad, received, wo, win_a, win_b, bin_a, bin_b, wout_a, wout_b,
    gain_1, shift_1, bias_out, gain_2, shift_2,
    o_act, o_first, o_ga, o_own, o_other, o_out,
    og, low_in, gb_all, gs_all, active, inner, vecs
):
    core = place[0]
    mine = pl.multiple_of(HALF * core, HALF)
    other = pl.multiple_of(HALF * (1 - core), HALF)
    hidden_units = win_a.shape[1]
    chunks = [(a, min(a + 256, hidden_units)) for a in range(0, hidden_units, 256)]
    halves = ((win_a, bin_a, wout_a), (win_b, bin_b, wout_b))
    low_in[:, 384:] = jnp.where(
        lax.broadcasted_iota(jnp.int32, (2 * SEG, 128), 1) == D - 384, 1.0, 0.0
    ).astype(LOW)
    gs_all[:, 384:] = jnp.zeros((2 * SEG, 128), LOW)
    vecs[...] = jnp.zeros_like(vecs)
    for s in range(2):
        og[s, pl.ds(mine, HALF)] = out_grad[2 * core + s]
        og[s, pl.ds(other, HALF)] = received[4 + s]
        rows = slice(SEG * s, SEG * s + SEG)
        hid = joined[s, MEM:].astype(F32)
        hat_1, scale_1 = norm_forward(hid + mm(att[s], wo[...]))
        first = hat_1 * gain_1[...] + shift_1[...]
        first_low = first.astype(LOW)
        low_in[rows, :D] = first_low
        ffn_sum = None
        slopes = []
        for which, (win, b_in, wout) in enumerate(halves):
            for a, z in chunks:
                pre = mm(first_low, win[:, a:z]) + b_in[:, a:z].astype(F32)
                act, slope = gelu_both(pre)
                act = act.astype(LOW)
                slopes.append(slope)
                active[which, rows, a:z] = act
                part = mm(act, wout[a:z])
                ffn_sum = part if ffn_sum is None else ffn_sum + part
        hat_2, scale_2 = norm_forward(first + ffn_sum + bias_out[...])
        o_act[s] = (hat_2 * gain_2[...] + shift_2[...]).astype(LOW)
        cot = og[s].astype(F32)
        vecs[2:3] += total_rows(cot * hat_2)
        vecs[3:4] += total_rows(cot)
        grad_second = norm_backward(cot * gain_2[...], hat_2, scale_2)
        vecs[4:5] += total_rows(grad_second)
        gs_low = grad_second.astype(LOW)
        gs_all[rows, :D] = gs_low
        grad_first = grad_second
        index = 0
        for which, (win, b_in, wout) in enumerate(halves):
            for a, z in chunks:
                grad_inner = (mm_nt(gs_low, wout[a:z]) * slopes[index]).astype(LOW)
                index += 1
                inner[which, rows, a:z] = grad_inner
                grad_first = grad_first + mm_nt(grad_inner, win[:, a:z])
        vecs[0:1] += total_rows(grad_first * hat_1)
        vecs[1:2] += total_rows(grad_first)
        grad_pre = norm_backward(grad_first * gain_1[...], hat_1, scale_1)
        o_first[s] = grad_pre
        grad_branch = grad_pre.astype(LOW)
        gb_all[rows] = grad_branch
        o_ga[s] = mm_nt(grad_branch, wo[...]).astype(LOW)
    in_t = low_in[...].T[:ROWS]
    gs_t = gs_all[...].T[:ROWS]
    for which, pack in ((1, o_other), (0, o_own)):
        for block in range(-(-hidden_units // 128)):
            a, z = 128 * block, min(128 * block + 128, hidden_units)
            pack[0, ROWS * block : ROWS * block + ROWS, : z - a] = mm(
                in_t, inner[which, :, a:z]
            ).astype(LOW)
            pack[1, ROWS * block : ROWS * block + ROWS, : z - a] = mm(
                gs_t, active[which, :, a:z]
            ).astype(LOW)
    grad_out = None
    for s in range(2):
        part = mm(att[s].T, gb_all[SEG * s : SEG * s + SEG])
        grad_out = part if grad_out is None else grad_out + part
    grad_out = mm(expander(ROWS), grad_out.astype(LOW))
    grad_out = grad_out + mm(pick_rows(8), vecs[...].astype(LOW))
    store_blocks(o_out, 0, grad_out)


def pick_rows(count):
    row = lax.broadcasted_iota(jnp.int32, (ROWS, count), 0)
    lane = lax.broadcasted_iota(jnp.int32, (ROWS, count), 1)
    return jnp.where((row == D + lane), 1.0, 0.0).astype(LOW)


def store_blocks(ref, base, values):
    low = values.astype(LOW)
    for block in range(4):
        a, z = 128 * block, min(128 * block + 128, D)
        ref[base + ROWS * block : base + ROWS * block + ROWS, : z - a] = low[:, a:z]


def back_kernel(
    probs, kv, uv, rel, ga, joined, wq, wkv, pos, first_grad, o_input, o_pack,
    scores, grel, dkv, wide, bias_sums
):
    pair = pl.program_id(0)
    stream = pl.program_id(1)
    flip = reversal(HALF)
    first_head = lax.broadcasted_iota(jnp.int32, (HALF, 128), 1) < 64
    zero = jnp.zeros((HALF, 128), LOW)
    key_rows = kv[0, 0, :, :128]
    value_rows = kv[0, 0, :, 128:]
    grad_att = ga[0]
    u_t = uv[0, 0, :, :128].T
    ga_t = grad_att.T

    @pl.when((pair == 0) & (stream == 0))
    def first_step():
        o_input[...] = first_grad[...]

    @pl.when(stream == 0)
    def clear():
        grel[...] = jnp.zeros_like(grel)
        bias_sums[pair] = jnp.zeros((8, 128), F32)

    grad_q = [None, None]
    sum_u = jnp.zeros((1, 128), F32)
    sum_v = jnp.zeros((1, 128), F32)
    for b in range(2):
        count = KEYS if b else KEYS - HALF
        width = count + HALF
        rows = slice(HALF * b, HALF * b + HALF)
        start_row = HALF - HALF * b
        v_t = mm(flip, uv[0, 0, rows, 128:]).astype(LOW).T
        parts = []
        for h in range(2):
            ga_h = jnp.where(first_head, grad_att[rows], zero) if h == 0 else jnp.where(
                first_head, zero, grad_att[rows]
            )
            grad_probs = mm_nt(ga_h, value_rows[:count])
            attn = probs[0, 0, h, rows, :count].astype(F32)
            inner = jnp.sum(grad_probs * attn, axis=1, keepdims=True)
            grad_scores = (attn * (grad_probs - inner)).astype(LOW)
            scores[h, rows, :count] = grad_scores
            if b == 0:
                scores[h, rows, count:] = jnp.zeros((HALF, HALF), LOW)
            turned = mm(flip, grad_scores)
            spread = jnp.concatenate([turned, jnp.zeros((HALF, HALF), F32)], axis=1)
            spread = pltpu.roll(spread, 0, 1, stride=1, stride_axis=0).astype(LOW)
            grad_u = mm(turned.astype(LOW), key_rows[:count])
            grad_v = mm(spread, rel[0, start_row : start_row + width])
            grel[64 * h : 64 * h + 64, start_row : start_row + width] += mm(
                v_t[64 * h : 64 * h + 64], spread
            )
            parts.append((grad_u, grad_v))
        grad_u = jnp.where(first_head, parts[0][0], parts[1][0]) * FACTOR
        grad_v = jnp.where(first_head, parts[0][1], parts[1][1]) * FACTOR
        sum_u = sum_u + total_rows(grad_u)
        sum_v = sum_v + total_rows(grad_v)
        grad_q[b] = mm(flip, (grad_u + grad_v).astype(LOW)).astype(LOW)
    bias_sums[pair, 0:1] += sum_u
    bias_sums[pair, 1:2] += sum_v
    for h in range(2):
        part = slice(64 * h, 64 * h + 64)
        dkv[part] = (mm(u_t[part], scores[h]) * FACTOR).astype(LOW)
        dkv[128 + 64 * h : 192 + 64 * h] = mm(ga_t[part], probs[0, 0, h]).astype(LOW)
    grad_queries = jnp.concatenate(grad_q, axis=0)
    token_grads = jnp.concatenate([grad_queries, dkv[:, MEM:].T], axis=1)
    token_weights = jnp.concatenate([wq[0], wkv[0]], axis=1)
    o_input[stream] += mm_nt(token_grads, token_weights)
    weight_kv = mm(dkv[...], joined[0])
    weight_q = mm(grad_queries.T, joined[0, MEM:])

    @pl.when(stream == 0)
    def store_first():
        wide[pair, :256] = weight_kv
        wide[pair, 256:384] = weight_q

    @pl.when(stream == 1)
    def store_second():
        wide[pair, :256] += weight_kv
        wide[pair, 256:384] += weight_q
        wide[pair, 384:512] = mm((grel[...] * FACTOR).astype(LOW), pos[...])

    @pl.when((pair == PAIRS - 1) & (stream == 1))
    def last_step():
        pick = expander(ROWS)
        back = compressor()
        for m in range(4):
            total = None
            for p in range(PAIRS):
                part = mm(
                    pick[:, 128 * p : 128 * p + 128], wide[p, 128 * m : 128 * m + 128].astype(LOW)
                )
                total = part if total is None else total + part
            if m == 2:
                vectors = None
                for p in range(PAIRS):
                    part = mm(bias_sums[p].astype(LOW), back[128 * p : 128 * p + 128])
                    vectors = part if vectors is None else vectors + part
                total = total + mm(pick_rows(8), vectors.astype(LOW))
            store_blocks(o_pack, 4 * ROWS * m, total)


def unpack_attention_kernel(pack_out, pack, o_out, o_key, o_value, o_query, o_pos, o_vec_a, o_vec_b):
    unit = identity(128)
    for block in range(4):
        a, z = 128 * block, min(128 * block + 128, D)
        part = pack_out[ROWS * block : ROWS * block + ROWS, : z - a].astype(F32)
        o_out[:, a:z] = part[:D]
        o_vec_a[:, a:z] = part[408:416]
        for m, ref in enumerate((o_key, o_value, o_query, o_pos)):
            base = 4 * ROWS * m + ROWS * block
            ref[a:z, :] = mm_nt(unit, pack[base : base + ROWS, :])[: z - a, :D]
            if m == 2:
                o_vec_b[:, a:z] = pack[base + 400 : base + ROWS, : z - a].astype(F32)[8:]


def unpack_ffn_kernel(pack, o_in, o_bias, o_out):
    unit = identity(128)
    units = o_in.shape[1]
    for block in range(-(-units // 128)):
        a, z = 128 * block, min(128 * block + 128, units)
        part = pack[0, ROWS * block : ROWS * block + ROWS, : z - a].astype(F32)
        o_in[:, a:z] = part[:D]
        o_bias[:, a:z] = part[408:416]
        o_out[a:z, :] = mm_nt(unit, pack[1, ROWS * block : ROWS * block + ROWS, :])[: z - a, :D]


def whole_spec():
    return pl.BlockSpec(memory_space=pltpu.VMEM)


def scalar_spec():
    return pl.BlockSpec(memory_space=pltpu.SMEM)


def params(**more):
    return pltpu.CompilerParams(vmem_limit_bytes=VMEM_BYTES, **more)


def cost(flops, moved):
    return pl.CostEstimate(flops=int(flops), bytes_accessed=int(moved), transcendentals=0)


def shape(dims, dtype=LOW):
    return jax.ShapeDtypeStruct(dims, dtype)


def prepare(w_query, w_key, w_value, w_pos, w_out, bias_u, bias_v, pos_table):
    return pl.pallas_call(
        prep_kernel,
        out_shape=(
            shape((PAIRS, D, 128)),
            shape((PAIRS, D, 256)),
            shape((PAIRS, SPAN, 128)),
            shape((WIDE, D)),
            shape((PAIRS, 2, 8, 128), F32),
        ),
        in_specs=[whole_spec()] * 8,
        out_specs=(whole_spec(),) * 5,
        compiler_params=params(),
        cost_estimate=cost(3e9, 5e6),
        name="prepare_weights",
    )(w_query, w_key, w_value, w_pos, w_out, bias_u[None], bias_v[None], pos_table)


def attend(place, seg_len, mem_len, hidden, memory, received, reset, wq, wkv, rel, bias):
    def fixed(dims):
        return pl.BlockSpec(dims, lambda s, p, *_: (0,) * len(dims))

    def paired(dims):
        return pl.BlockSpec((1,) + dims, lambda s, p, *_: (p,) + (0,) * len(dims))

    def both(dims):
        return pl.BlockSpec((1, 1) + dims, lambda s, p, *_: (s, p) + (0,) * len(dims))

    return pl.pallas_call(
        attend_kernel,
        grid_spec=pltpu.PrefetchScalarGridSpec(
            num_scalar_prefetch=3,
            grid=(2, PAIRS),
            in_specs=[
                fixed(hidden.shape),
                fixed(memory.shape),
                fixed(received.shape),
                fixed(reset.shape),
                paired((D, 128)),
                paired((D, 256)),
                paired((SPAN, 128)),
                paired((2, 8, 128)),
            ],
            out_specs=[
                both((2, SEG, KEYS)),
                both((KEYS, 256)),
                both((SEG, 256)),
                pl.BlockSpec((1, SEG, 128), lambda s, p, *_: (s, 0, p)),
                pl.BlockSpec((1, KEYS, D), lambda s, p, *_: (s, 0, 0)),
            ],
            scratch_shapes=[pltpu.VMEM((SEG, KEYS), F32)],
        ),
        out_shape=(
            shape((2, PAIRS, 2, SEG, KEYS)),
            shape((2, PAIRS, KEYS, 256)),
            shape((2, PAIRS, SEG, 256)),
            shape((2, SEG, WIDE)),
            shape((2, KEYS, D)),
        ),
        compiler_params=params(),
        cost_estimate=cost(8e9, 12e6),
        name="attend",
    )(place, seg_len, mem_len, hidden, memory, received, reset, wq, wkv, rel, bias)


def feed_forward(place, att, joined, out_grad, received, wo, own, other, vectors):
    units = own[0].shape[1]
    blocks = -(-units // 128)
    weights = (own[0], other[0], own[1], other[1], own[2], other[2])
    return pl.pallas_call(
        ffn_kernel,
        out_shape=(
            shape((2, SEG, D)),
            shape((2, SEG, D), F32),
            shape((2, SEG, WIDE)),
            shape((2, ROWS * blocks, 128)),
            shape((2, ROWS * blocks, 128)),
            shape((4 * ROWS, 128)),
        ),
        in_specs=[scalar_spec()] + [whole_spec()] * 16,
        out_specs=(whole_spec(),) * 6,
        scratch_shapes=[
            pltpu.VMEM((2, SEG, D), LOW),
            pltpu.VMEM((2 * SEG, 512), LOW),
            pltpu.VMEM((2 * SEG, D), LOW),
            pltpu.VMEM((2 * SEG, 512), LOW),
            pltpu.VMEM((2, 2 * SEG, units), LOW),
            pltpu.VMEM((2, 2 * SEG, units), LOW),
            pltpu.VMEM((8, D), F32),
        ],
        compiler_params=params(),
        cost_estimate=cost(1e10, 15e6),
        name="feed_forward",
    )(place, att, joined, out_grad, received, wo, *weights, *vectors)


def attend_back(probs, kv, uv, rel, ga, joined, wq, wkv, pos_table, first_grad):
    def fixed(dims):
        return pl.BlockSpec(dims, lambda p, s: (0,) * len(dims))

    def paired(dims):
        return pl.BlockSpec((1,) + dims, lambda p, s: (p,) + (0,) * len(dims))

    def both(dims):
        return pl.BlockSpec((1, 1) + dims, lambda p, s: (s, p) + (0,) * len(dims))

    return pl.pallas_call(
        back_kernel,
        grid=(PAIRS, 2),
        in_specs=[
            both((2, SEG, KEYS)),
            both((KEYS, 256)),
            both((SEG, 256)),
            paired((SPAN, 128)),
            pl.BlockSpec((1, SEG, 128), lambda p, s: (s, 0, p)),
            pl.BlockSpec((1, KEYS, D), lambda p, s: (s, 0, 0)),
            paired((D, 128)),
            paired((D, 256)),
            fixed((SPAN, D)),
            fixed((2, SEG, D)),
        ],
        out_specs=[fixed((2, SEG, D)), fixed((16 * ROWS, 128))],
        out_shape=(shape((2, SEG, D), F32), shape((16 * ROWS, 128))),
        scratch_shapes=[
            pltpu.VMEM((2, SEG, KEYS), LOW),
            pltpu.VMEM((128, SPAN), F32),
            pltpu.VMEM((256, KEYS), LOW),
            pltpu.VMEM((PAIRS, 512, D), F32),
            pltpu.VMEM((PAIRS, 8, 128), F32),
        ],
        compiler_params=params(),
        cost_estimate=cost(1.5e10, 15e6),
        name="attend_back",
    )(probs, kv, uv, rel, ga, joined, wq, wkv, pos_table, first_grad)


def unpack_attention(pack_out, pack):
    return pl.pallas_call(
        unpack_attention_kernel,
        out_shape=(shape((D, D), F32),) * 5 + (shape((8, D), F32),) * 2,
        in_specs=[whole_spec()] * 2,
        out_specs=(whole_spec(),) * 7,
        compiler_params=params(),
        name="unpack_attention",
    )(pack_out, pack)


def unpack_ffn(pack, units):
    return pl.pallas_call(
        unpack_ffn_kernel,
        out_shape=(shape((D, units), F32), shape((8, units), F32), shape((units, D), F32)),
        in_specs=[whole_spec()],
        out_specs=(whole_spec(),) * 3,
        compiler_params=params(),
        name="unpack_ffn",
    )(pack)


def swap(values):
    return lax.ppermute(values, "tp", [(0, 1), (1, 0)])


def bits_of(count):
    return [k for k in range(count.bit_length() - 1)]


def reduce_halves(values, bits, axis_size, index):
    for k in bits:
        rows = values.shape[0] // 2
        bit = (index >> k) & 1
        sent = lax.dynamic_slice_in_dim(values, (1 - bit) * rows, rows, 0)
        kept = lax.dynamic_slice_in_dim(values, bit * rows, rows, 0)
        values = kept + lax.ppermute(
            sent, "dp", [(i, i ^ (1 << k)) for i in range(axis_size)]
        )
    return values


def gather_halves(values, bits, axis_size, index):
    for k in reversed(bits):
        came = lax.ppermute(values, "dp", [(i, i ^ (1 << k)) for i in range(axis_size)])
        bit = (index >> k) & 1
        values = jnp.where(
            bit == 0,
            jnp.concatenate([values, came], axis=0),
            jnp.concatenate([came, values], axis=0),
        )
    return values


def padded_rows(values, multiple):
    extra = -values.shape[0] % multiple
    return jnp.pad(values, ((0, extra), (0, 0))) if extra else values


def make_shards(dp_size):
    table = position_table()

    def shards(
        hidden, memory, segment_length, memory_length, doc_reset, w_query, w_key, w_value, w_pos,
        bias_u, bias_v, w_out, first_gain, first_shift, ffn_in, ffn_in_bias, ffn_out, ffn_out_bias,
        second_gain, second_shift, out_grad,
    ):
        core = lax.axis_index("tp")
        index = lax.axis_index("dp")
        place = core[None].astype(jnp.int32)
        units = ffn_in.shape[1]
        pos_table = jnp.asarray(table)

        def halves(values, which):
            return lax.dynamic_slice_in_dim(values, 2 * which, 2, 0)

        sent = jnp.concatenate([halves(a, 1 - core) for a in (hidden, memory, out_grad)], axis=0)
        received = swap(sent)
        other_ffn = (swap(ffn_in), swap(ffn_in_bias[None]), swap(ffn_out))
        own_ffn = (ffn_in, ffn_in_bias[None], ffn_out)

        wq, wkv, rel, wo, bias = prepare(
            w_query, w_key, w_value, w_pos, w_out, bias_u, bias_v, pos_table
        )
        probs, kv, uv, att, joined = attend(
            place, segment_length, memory_length, hidden, memory, received, doc_reset,
            wq, wkv, rel, bias,
        )
        act, first_grad, ga, ffn_own, ffn_other, pack_out = feed_forward(
            place, att, joined, out_grad, received, wo, own_ffn, other_ffn,
            tuple(v[None] for v in (first_gain, first_shift, ffn_out_bias, second_gain, second_shift)),
        )
        bits = bits_of(dp_size)
        ffn_total = (ffn_own + swap(ffn_other)).reshape(-1, 128)
        ffn_rows = ffn_total.shape[0]
        ffn_total = padded_rows(ffn_total, 16 * dp_size)
        ffn_total = gather_halves(
            reduce_halves(ffn_total, bits, dp_size, index), bits, dp_size, index
        )[:ffn_rows]
        grad_in, grad_in_bias, grad_ffn_out = unpack_ffn(ffn_total.reshape(2, -1, 128), units)

        input_own, pack = attend_back(
            probs, kv, uv, rel, ga, joined, wq, wkv, pos_table, first_grad
        )
        total = jnp.concatenate([pack_out, pack], axis=0)
        total_count = total.shape[0]
        total = padded_rows(total, 32 * dp_size)
        half = total.shape[0] // 2
        kept = lax.dynamic_slice_in_dim(total, core * half, half, 0)
        total = kept + swap(lax.dynamic_slice_in_dim(total, (1 - core) * half, half, 0))
        total = gather_halves(
            reduce_halves(total, bits, dp_size, index), bits, dp_size, index
        )
        came = swap(total)
        total = jnp.where(
            core == 0,
            jnp.concatenate([total, came], axis=0),
            jnp.concatenate([came, total], axis=0),
        )[:total_count]
        g_out, g_key, g_value, g_query, g_pos, vec_a, vec_b = unpack_attention(
            total[: 4 * ROWS], total[4 * ROWS :]
        )

        def give_back(values, dtype):
            rows = values.shape[1] // 2
            mine = lax.dynamic_slice_in_dim(values, core * rows, rows, 1)
            theirs = lax.dynamic_slice_in_dim(values, (1 - core) * rows, rows, 1)
            came = swap(theirs.astype(LOW)).astype(dtype)
            mine = mine.astype(dtype)
            return jnp.where(
                core == 0,
                jnp.concatenate([mine, came], axis=0),
                jnp.concatenate([came, mine], axis=0),
            )

        activations = give_back(act, LOW)
        input_grad = give_back(input_own, F32)

        rows = hidden.shape[1]
        positions = core * rows + jnp.arange(rows)
        later = (jnp.arange(SEG)[:, None] > positions[None, :]).astype(LOW)
        resets = jnp.dot(doc_reset.astype(LOW), later, preferred_element_type=F32)
        keep = (resets == 0.0) & (positions[None, :] < segment_length[:, None])
        new_memory = jnp.where(keep[:, :, None], hidden, jnp.zeros_like(hidden))
        return (
            new_memory, activations, input_grad, g_query, g_key, g_value, g_pos,
            vec_b[2], vec_b[3], g_out, vec_a[2], vec_a[3],
            grad_in, grad_in_bias[2], grad_ffn_out, vec_a[6], vec_a[4], vec_a[5],
        )

    return shards


def solution(mesh):
    rows, copied = P("dp", "tp", None), P()
    shards = make_shards(mesh.shape["dp"])
    return jax.shard_map(
        shards,
        mesh=mesh,
        in_specs=(
            rows, rows, P("dp"), P("dp"), P("dp", None),
            copied, copied, copied, copied, copied, copied, copied, copied, copied,
            P(None, "tp"), P("tp"), P("tp", None),
            copied, copied, copied, rows,
        ),
        out_specs=(
            rows, rows, rows, copied, copied, copied, copied, copied, copied, copied, copied, copied,
            P(None, "tp"), P("tp"), P("tp", None), copied, copied, copied,
        ),
        check_vma=False,
    )
```

time: 625 us -> 263 us (0.42); the launches traced: 614 us -> 262 us
  local copies, waits for them, and re-layouts: 203 us -> 26.1 us
  waiting for transfers between devices: 208 us -> 65.1 us
  Pallas kernels: 0 us -> 118 us
  blocking collectives: 90.5 us -> 0 us
  matrix products: 73.4 us -> 0.15 us
  starting transfers between devices: 0.79 us -> 26.1 us
  between operations: 16.7 us -> 1.26 us
    psum x2 -> x0, waiting for transfers between devices: 206 us -> none  [the longest x1 162 us: shards(): ffn_grads = lax.psum((ffn_grads[0], ffn_grads[1], ffn_grads[2]), 'dp')]
    pallas_call x0 -> x6, Pallas kernels: none -> 118 us  [the longest x1 42 us: attend_back(): pl.pallas_call(back_kernel, grid=(PAIRS, 2), in_specs=[both((2, SEG, KEYS...]
    psum x2 -> x0, blocking collectives: 85.5 us -> none  [the longest x1 42.8 us: shards(): lax.psum((grad_query_w, grad_pair_w, grad_pos_w, grad_out_w, jnp.sum(grad...]
    dot_general x26 -> x1, matrix products: 73.4 us -> 0.15 us  [shards(): resets = jnp.dot(doc_reset.astype(LOW), later, preferred_element_type=F32)]
    reshape x6 -> x0, local copies, waits for them, and re-layouts: 72.3 us -> none  [the longest x1 20.1 us: shift_rows(): flat_rows.reshape(leading + (row_count, span_rows - 1))[..., :key_count]]
    ppermute x0 -> x25, waiting for transfers between devices: none -> 65.1 us  [the longest x8 43 us: reduce_halves(): lax.ppermute(sent, 'dp', [(i, i ^ 1 << k) for i in range(axis_size)])]
    unnamed x149 -> x36, local copies, waits for them, and re-layouts: 56.4 us -> 10.6 us
    ppermute x0 -> x25, starting transfers between devices: none -> 26.1 us  [the longest x8 15.5 us: reduce_halves(): lax.ppermute(sent, 'dp', [(i, i ^ 1 << k) for i in range(axis_size)])]
  transfers between devices with their start and end apart: 9 -> 25, of which waited for: 2 -> 14; matrix products, arithmetic and copies ran while one was open for 38% -> 14% of each run, Pallas kernels for 0% -> 14%
where the time goes in v1:
time: 263 us; the launch traced here: 262 us
  Pallas kernels  118 us (45%)
  waiting for transfers between devices  65.1 us (25%)
  local copies, waits for them, and re-layouts  26.1 us (10%)
  starting transfers between devices  26.1 us (10%)
  other arithmetic  25.7 us (10%)
    ppermute x8, waiting for transfers between devices, reduce_halves(): lax.ppermute(sent, 'dp', [(i, i ^ 1 << k) for i in range(axis_size)])  43 us
    pallas_call x1, Pallas kernels, attend_back(): pl.pallas_call(back_kernel, grid=(PAIRS, 2), in_specs=[both((2, SEG, KEYS...  42 us
    pallas_call x1, Pallas kernels, feed_forward(): pl.pallas_call(ffn_kernel, out_shape=(shape((2, SEG, D)), shape((2, SEG,...  34.6 us
    pallas_call x1, Pallas kernels, attend(): pl.pallas_call(attend_kernel, grid_spec=pltpu.PrefetchScalarGridSpec(num_...  27.1 us
    ppermute x8, waiting for transfers between devices, gather_halves(): lax.ppermute(values, 'dp', [(i, i ^ 1 << k) for i in range(axis_size)])  18.6 us
    ppermute x8, starting transfers between devices, reduce_halves(): lax.ppermute(sent, 'dp', [(i, i ^ 1 << k) for i in range(axis_size)])  15.5 us
    unnamed x36, local copies, waits for them, and re-layouts  10.6 us
    select_n x1, other arithmetic, shards(): jnp.where(core == 0, jnp.concatenate([total, came], axis=0), jnp.concaten...  9.04 us
  transfers between devices with their start and end apart: 25, of which 14 were waited for; matrix products, arithmetic and copies ran while one was open for 14% of the time, Pallas kernels for 14%

profile of v1, /device:TPU:0, one launch (start us, length us, event | category | flops | bytes accessed | tf_op | source)
XLA Modules:
  0.0 262.3 jit_solution(14018818934830497862)
XLA Ops:
  0.7 1.7 constant_dynamic-slice_fusion.11
  2.4 1.2 constant_dynamic-slice_fusion.13
  3.7 0.9 pad_maximum_fusion.2
  4.6 0.5 collective-permute-start
  5.2 0.5 collective-permute-start.3
  5.7 5.9 %prepare_weights.1 = (bf16[5,410,128]{2,1,0:T(8,128)(2,1)}, bf16[5,410,256]{2,1,0:T(8,128)(2,1)}, bf16[5,768,128]{2,1,0:T(8,128)(2,1)}, bf16[640,410]{1,0:T(8,128)(2,1)}, f32[5,2,8,128]{3,2,1,0:T(8,128)}) custom-call(bf16[410,410]{1,0:T(8,128)(2,1)} %wq.1, bf16[410,410]{1,0:T(8,128)(2,1)} %wk.1, bf16[410,410]{1,0:T(8,128)(2,1)} %wv.1, bf16[410,410]{1,0:T(8,128)(2,1)} %wp.1, ...), custom_call_target="tpu_custom_call" | custom-call | flops 3000000000 | bytes 5000000 | tf_op jit(solution)/shard_map/prepare_weights/pallas_call | solution.py:438
  11.6 1.1 copy.54.hidden
  12.7 1.1 copy.55.memory
  13.8 1.5 copy.59.wout_a
  15.3 1.1 copy.57.out_grad
  16.4 2.2 copy.56.received
  18.7 27.1 %attend.1 = (bf16[2,5,2,256,512]{4,3,2,1,0:T(8,128)(2,1)}, bf16[2,5,512,256]{3,2,1,0:T(8,128)(2,1)}, bf16[2,5,256,256]{3,2,1,0:T(8,128)(2,1)}, bf16[2,256,640]{2,1,0:T(8,128)(2,1)}, bf16[2,512,410]{2,1,0:T(8,128)(2,1)}) custom-call(s32[1]{0:T(128)} %bitcast.1.place, s32[4]{0:T(128)} %seg_len.1, s32[4]{0:T(128)} %mem_len.1, ...), custom_call_target="tpu_custom_call" | custom-call | flops 8000000000 | bytes 12000000 | tf_op jit(solution)/shard_map/attend/pallas_call | solution.py:465
  45.7 1.8 copy.60.wout_b
  47.5 0.6 copy-done.10
  48.1 34.6 %feed_forward.1 = (bf16[2,256,410]{2,1,0:T(8,128)(2,1)}, f32[2,256,410]{2,1,0:T(8,128)}, bf16[2,256,640]{2,1,0:T(8,128)(2,1)}, bf16[2,3744,128]{2,1,0:T(8,128)(2...) custom-call(s32[1]{0:T(128)} %bitcast.1.place, bf16[2,256,640]{2,1,0:T(8,128)(2,1)} %get-tuple-element.50.att, ...), custom_call_target="tpu_custom_call" | custom-call | flops 10000000000 | bytes 15000000 | tf_op jit(solution)/shard_map/feed_forward/pallas_call | solution.py:506
  82.7 42.0 %attend_back.1 = (f32[2,256,410]{2,1,0:T(8,128)}, bf16[6656,128]{1,0:T(8,128)(2,1)}) custom-call(bf16[2,5,2,256,512]{4,3,2,1,0:T(8,128)(2,1)} %get-tuple-element.54.probs, bf16[2,5,512,256]{3,2,1,0:T(8,128)(2,1)} %get-tuple-element.55.kv, bf16[2,5,256,256]{3,2,1,0:T(8,128)(2,1)} %get-tuple-element.56.uv, bf16[5,768,128]{2,1,0:T(8,128)(2,1)} %get-tuple-element.48.rel, ...), custom_call_target="tpu_custom_call" | custom-call | flops 15000000512 | bytes 15000000 | tf_op jit(solution)/shard_map/attend_back/pallas_call | solution.py:543
  124.7 3.6 %fusion.2 = bf16[8704,128]{1,0:T(8,128)(2,1)S(1)} fusion(bf16[6656,128]{1,0:T(8,128)(2,1)} %get-tuple-element.61, bf16[1664,128]{1,0:T(8,128)(2,1)S(1)} %copy-done.7), kind=kLoop, calls=%fused_computation.3 | loop fusion | flops 7798784 | bytes 4358144 | tf_op jit(solution)/shard_map/concatenate | solution.py:677
  128.4 0.5 collective-permute-start.6
  129.0 3.1 %collective-permute-done.6 = bf16[4352,128]{1,0:T(8,128)(2,1)} collective-permute-done((bf16[4352,128]{1,0:T(8,128)(2,1)S(1)}, bf16[4352,128]{1,0:T(8,128)(2,1)}, u32[]{:S(2)}, u32[]{:S(2)}) %collective-permute-start.6) | collective-permute-done | bytes 1114144 | tf_op jit(solution)/shard_map/ppermute | solution.py:596
  132.1 1.5 dynamic-slice_add_fusion
  133.7 2.9 %collective-permute-start.7 = (bf16[2176,128]{1,0:T(8,128)(2,1)S(1)}, bf16[2176,128]{1,0:T(8,128)(2,1)S(1)}, u32[]{:S(2)}, u32[]{:S(2)}) collective-permute-start(bf16[2176,128]{1,0:T(8,128)(2,1)S(1)} %constant_dynamic-slice_fusion.6), channel_id=1, source_target_pairs={{0,2},{2,0},{4,6},{6,4},{8,10},{10,8},{12,14},{14,12},{16,18},{18,... | collective-permute-start | bytes 1671176 | tf_op jit(solution)/shard_map/ppermute | solution.py:609
  136.6 12.9 %collective-permute-done.7 = bf16[2176,128]{1,0:T(8,128)(2,1)S(1)} collective-permute-done((bf16[2176,128]{1,0:T(8,128)(2,1)S(1)}, bf16[2176,128]{1,0:T(8,128)(2,1)S(1)}, u32[]{:S(2)}, u32[]{:S(2)}) %collective-permute-start.7) | collective-permute-done | bytes 557088 | tf_op jit(solution)/shard_map/ppermute | solution.py:609
  149.7 1.8 collective-permute-start.8
  151.5 2.6 add.131
  154.2 1.6 collective-permute-start.17
  155.9 2.1 collective-permute-done.8
  158.1 1.6 collective-permute-start.9
  159.6 3.5 %collective-permute-done.9 = bf16[544,128]{1,0:T(8,128)(2,1)S(1)} collective-permute-done((bf16[544,128]{1,0:T(8,128)(2,1)S(1)}, bf16[544,128]{1,0:T(8,128)(2,1)S(1)}, u32[]{:S(2)}, u32[]{:S(2)}) %collective-permute-start.9) | collective-permute-done | bytes 139296 | tf_op jit(solution)/shard_map/ppermute | solution.py:609
  163.3 2.6 collective-permute-start.10
  165.9 11.3 %collective-permute-done.17 = bf16[3840,128]{1,0:T(8,128)(2,1)} collective-permute-done((bf16[3840,128]{1,0:T(8,128)(2,1)S(1)}, bf16[3840,128]{1,0:T(8,128)(2,1)}, u32[]{:S(2)}, u32[]{:S(2)}) %collective-permute-start.17) | collective-permute-done | bytes 983072 | tf_op jit(solution)/shard_map/ppermute | solution.py:609
  177.1 1.5 fusion.6
  178.7 0.7 collective-permute-start.18
  179.4 2.6 collective-permute-start.11
  182.0 2.7 %collective-permute-done.11 = bf16[272,128]{1,0:T(8,128)(2,1)S(1)} collective-permute-done((bf16[272,128]{1,0:T(8,128)(2,1)S(1)}, bf16[272,128]{1,0:T(8,128)(2,1)S(1)}, u32[]{:S(2)}, u32[]{:S(2)}) %collective-permute-start.11) | collective-permute-done | bytes 69664 | tf_op jit(solution)/shard_map/ppermute | solution.py:617
  184.7 1.6 collective-permute-start.12
  186.3 3.8 %collective-permute-done.18 = bf16[1920,128]{1,0:T(8,128)(2,1)} collective-permute-done((bf16[1920,128]{1,0:T(8,128)(2,1)S(1)}, bf16[1920,128]{1,0:T(8,128)(2,1)}, u32[]{:S(2)}, u32[]{:S(2)}) %collective-permute-start.18) | collective-permute-done | bytes 491552 | tf_op jit(solution)/shard_map/ppermute | solution.py:609
  190.1 1.2 dynamic-slice_add_fusion.2
  191.3 1.7 collective-permute-start.19
  193.2 0.6 collective-permute-start.13
  193.8 5.1 %collective-permute-done.19 = bf16[960,128]{1,0:T(8,128)(2,1)S(1)} collective-permute-done((bf16[960,128]{1,0:T(8,128)(2,1)S(1)}, bf16[960,128]{1,0:T(8,128)(2,1)S(1)}, u32[]{:S(2)}, u32[]{:S(2)}) %collective-permute-start.19) | collective-permute-done | bytes 245792 | tf_op jit(solution)/shard_map/ppermute | solution.py:609
  198.9 2.7 %collective-permute-start.20 = (bf16[480,128]{1,0:T(8,128)(2,1)S(1)}, bf16[480,128]{1,0:T(8,128)(2,1)S(1)}, u32[]{:S(2)}, u32[]{:S(2)}) collective-permute-start(bf16[480,128]{1,0:T(8,128)(2,1)S(1)} %constant_dynamic-slice_fusion), channel_id=1, source_target_pairs={{0,16},{2,18},{4,20},{6,22},{8,24},{10,26},{12,28},{14,30},{16,0},... | collective-permute-start | bytes 368648 | tf_op jit(solution)/shard_map/ppermute | solution.py:609
  201.8 1.5 collective-permute-start.14
  203.2 4.3 %collective-permute-done.20 = bf16[480,128]{1,0:T(8,128)(2,1)S(1)} collective-permute-done((bf16[480,128]{1,0:T(8,128)(2,1)S(1)}, bf16[480,128]{1,0:T(8,128)(2,1)S(1)}, u32[]{:S(2)}, u32[]{:S(2)}) %collective-permute-start.20) | collective-permute-done | bytes 122912 | tf_op jit(solution)/shard_map/ppermute | solution.py:609
  207.7 0.9 broadcast_select_fusion
  208.7 1.1 dynamic-slice_convert_fusion
  209.8 4.9 %collective-permute-done.21 = bf16[480,128]{1,0:T(8,128)(2,1)S(1)} collective-permute-done((bf16[480,128]{1,0:T(8,128)(2,1)S(1)}, bf16[480,128]{1,0:T(8,128)(2,1)S(1)}, u32[]{:S(2)}, u32[]{:S(2)}) %collective-permute-start.21) | collective-permute-done | bytes 122912 | tf_op jit(solution)/shard_map/ppermute | solution.py:617
  215.3 5.8 %collective-permute-done.22 = bf16[960,128]{1,0:T(8,128)(2,1)S(1)} collective-permute-done((bf16[960,128]{1,0:T(8,128)(2,1)S(1)}, bf16[960,128]{1,0:T(8,128)(2,1)S(1)}, u32[]{:S(2)}, u32[]{:S(2)}) %collective-permute-start.22) | collective-permute-done | bytes 245792 | tf_op jit(solution)/shard_map/ppermute | solution.py:617
  221.2 0.8 collective-permute-start.23
  222.0 0.7 constant_dynamic-slice_fusion.10
  223.0 1.2 copy.62
  224.7 1.2 maximum_select_fusion.5
  225.8 1.0 copy.61
  226.8 4.9 %collective-permute-done.23 = bf16[1920,128]{1,0:T(8,128)(2,1)S(1)} collective-permute-done((bf16[1920,128]{1,0:T(8,128)(2,1)S(1)}, bf16[1920,128]{1,0:T(8,128)(2,1)S(1)}, u32[]{:S(2)}, u32[]{:S(2)}) %collective-permute-start.23) | collective-permute-done | bytes 491552 | tf_op jit(solution)/shard_map/ppermute | solution.py:617
  232.0 1.4 collective-permute-start.24
  233.4 9.0 %maximum_select_fusion = bf16[8704,128]{1,0:T(8,128)(2,1)S(1)} fusion(bf16[4352,128]{1,0:T(8,128)(2,1)} %collective-permute-done.15, bf16[4352,128]{1,0:T(8,128)(2,1)S(1)} %maximum_select_fusion.1, pred[]{:T(512)S(6)} %eq.33), kind=kLoop, calls=%fused_computation.4 | loop fusion | flops 10027008 | bytes 4456449 | tf_op jit(solution)/shard_map/jit(_where)/select_n | solution.py:687
  242.4 1.3 slice.48.pack
  243.7 0.8 slice.47.pack_out
  244.5 4.3 %unpack_attention.1 = (f32[410,410]{1,0:T(8,128)}, f32[410,410]{1,0:T(8,128)}, f32[410,410]{1,0:T(8,128)}, f32[410,410]{1,0:T(8,128)}, f32[410,410]{1,0:T(8,128)}, /*index=5*/f32[8,410]{1,0:T(8,128)}, f32[8,410]{1,0:T(8,128)}) custom-call(bf16[1664,128]{1,0:T(8,128)(2,1)} %slice.47.pack_out, bf16[6656,128]{1,0:T(8,128)(2,1)} %slice.48.pack), custom_call_target="tpu_custom_call" | custom-call | tf_op jit(solution)/shard_map/unpack_attention/pallas_call | solution.py:574
  248.8 1.4 fusion.10
  250.2 1.5 fusion.9
  252.0 1.8 fusion.3
  253.8 4.1 %unpack_ffn.1 = (f32[410,1050]{1,0:T(8,128)}, f32[8,1050]{1,0:T(8,128)}, f32[1050,410]{1,0:T(8,128)}) custom-call(bf16[2,3744,128]{2,1,0:T(8,128)(2,1)} %bitcast.23), custom_call_target="tpu_custom_call" | custom-call | tf_op jit(solution)/shard_map/unpack_ffn/pallas_call | solution.py:585
  257.9 2.9 %copy.63 = f32[1050,410]{0,1:T(8,128)} copy(f32[1050,410]{1,0:T(8,128)} %get-tuple-element.106) | data formatting | bytes 3444000
  260.7 1.4 slice_reduce_fusion
  (77 shorter events, 3.8 us)
Async XLA Ops:
  0.7 4.4 %copy-start.9 = (bf16[1050]{0:T(1024)(128)(2,1)S(1)}, bf16[1050]{0:T(1024)(128)(2,1)}, u32[]{:S(2)}) copy-start(bf16[1050]{0:T(1024)(128)(2,1)} %param.37) | copy-start | bytes 6304
  0.7 4.5 %copy-start.2 = (bf16[1050,410]{0,1:T(8,128)(2,1)S(1)}, bf16[1050,410]{0,1:T(8,128)(2,1)}, u32[]{:S(2)}) copy-start(bf16[1050,410]{0,1:T(8,128)(2,1)} %param.38) | copy-start | bytes 2583004
  4.6 11.8 %collective-permute-start = (bf16[6,128,410]{1,2,0:T(8,128)(2,1)}, bf16[6,128,410]{1,2,0:T(8,128)(2,1)}, u32[]{:S(2)}, u32[]{:S(2)}) collective-permute-start(bf16[6,128,410]{1,2,0:T(8,128)(2,1)} %pad_maximum_fusion.2), channel_id=1, source_target_pairs={{0,1},{1,0},{2,3},{3,2},{4,5},{5,4},{6,7},{7,6},{8,9},{9,8},{10,11... | collective-permute-start | bytes 1889288 | tf_op jit(solution)/shard_map/ppermute | solution.py:596
  5.1 6.5 %copy-start.8 = (bf16[1,1050]{1,0:T(2,128)(2,1)}, bf16[1,1050]{1,0:T(2,128)(2,1)S(1)}, u32[]{:S(2)}) copy-start(bf16[1,1050]{1,0:T(2,128)(2,1)S(1)} %broadcast_in_dim.49.bin_a) | copy-start | bytes 6304
  5.1 42.4 %collective-permute-start.2 = (bf16[1,1050]{1,0:T(2,128)(2,1)S(1)}, bf16[1,1050]{1,0:T(2,128)(2,1)S(1)}, u32[]{:S(2)}, u32[]{:S(2)}) collective-permute-start(bf16[1,1050]{1,0:T(2,128)(2,1)S(1)} %broadcast_in_dim.49.bin_a), channel_id=1, source_target_pairs={{0,1},{1,0},{2,3},{3,2},{4,5},{5,4},{6,7},{7,6},{8,9},{9,8},{10,11... | collective-permute-start | bytes 6308 | tf_op jit(solution)/shard_map/ppermute | solution.py:596
  5.2 40.5 %collective-permute-start.3 = (bf16[1050,410]{0,1:T(8,128)(2,1)S(1)}, bf16[1050,410]{0,1:T(8,128)(2,1)S(1)}, u32[]{:S(2)}, u32[]{:S(2)}) collective-permute-start(bf16[1050,410]{0,1:T(8,128)(2,1)S(1)} %copy-done.2), channel_id=1, source_target_pairs={{0,1},{1,0},{2,3},{3,2},{4,5},{5,4},{6,7},{7,6},{8,9},{9,8},{10,11... | collective-permute-start | bytes 2583008 | tf_op jit(solution)/shard_map/ppermute | solution.py:596
  5.7 41.9 %collective-permute-start.1 = (bf16[410,1050]{1,0:T(8,128)(2,1)}, bf16[410,1050]{1,0:T(8,128)(2,1)}, u32[]{:S(2)}, u32[]{:S(2)}) collective-permute-start(bf16[410,1050]{1,0:T(8,128)(2,1)} %win_a.1), channel_id=1, source_target_pairs={{0,1},{1,0},{2,3},{3,2},{4,5},{5,4},{6,7},{7,6},{8,9},{9,8},{10,11... | collective-permute-start | bytes 2583008 | tf_op jit(solution)/shard_map/ppermute | solution.py:596
  5.7 5.9 %copy-start = (bf16[4,128,410]{1,0,2:T(4,128)(2,1)S(1)}, bf16[4,128,410]{1,0,2:T(4,128)(2,1)}, u32[]{:S(2)}) copy-start(bf16[4,128,410]{1,0,2:T(4,128)(2,1)} %param.22) | copy-start | bytes 1259524
  5.7 7.0 %copy-start.3 = (bf16[4,128,410]{1,0,2:T(4,128)(2,1)S(1)}, bf16[4,128,410]{1,0,2:T(4,128)(2,1)}, u32[]{:S(2)}) copy-start(bf16[4,128,410]{1,0,2:T(4,128)(2,1)} %param.23) | copy-start | bytes 1259524
  11.6 3.7 %copy-start.4 = (bf16[4,128,410]{1,0,2:T(4,128)(2,1)S(1)}, bf16[4,128,410]{1,0,2:T(4,128)(2,1)}, u32[]{:S(2)}) copy-start(bf16[4,128,410]{1,0,2:T(4,128)(2,1)} %param.42) | copy-start | bytes 1259524
  47.5 0.6 copy-start.10
  82.7 42.0 %copy-start.7 = (bf16[1664,128]{1,0:T(8,128)(2,1)S(1)}, bf16[1664,128]{1,0:T(8,128)(2,1)}, u32[]{:S(2)}) copy-start(bf16[1664,128]{1,0:T(8,128)(2,1)} %get-tuple-element.60) | copy-start | bytes 1277956
  128.4 3.7 %collective-permute-start.6 = (bf16[4352,128]{1,0:T(8,128)(2,1)S(1)}, bf16[4352,128]{1,0:T(8,128)(2,1)}, u32[]{:S(2)}, u32[]{:S(2)}) collective-permute-start(bf16[4352,128]{1,0:T(8,128)(2,1)S(1)} %constant_dynamic-slice_fusion.7), channel_id=1, source_target_pairs={{0,1},{1,0},{2,3},{3,2},{4,5},{5,4},{6,7},{7,6},{8,9},{9,8},{10,11... | collective-permute-start | bytes 3342344 | tf_op jit(solution)/shard_map/ppermute | solution.py:596
  128.9 22.6 %collective-permute-start.16 = (bf16[2,3744,128]{2,1,0:T(8,128)(2,1)}, bf16[2,3744,128]{2,1,0:T(8,128)(2,1)}, u32[]{:S(2)}, u32[]{:S(2)}) collective-permute-start(bf16[2,3744,128]{2,1,0:T(8,128)(2,1)} %get-tuple-element.70), channel_id=1, source_target_pairs={{0,1},{1,0},{2,3},{3,2},{4,5},{5,4},{6,7},{7,6},{8,9},{9,8},{10,11... | collective-permute-start | bytes 5750792 | tf_op jit(solution)/shard_map/ppermute | solution.py:596
  133.7 15.9 %collective-permute-start.7 = (bf16[2176,128]{1,0:T(8,128)(2,1)S(1)}, bf16[2176,128]{1,0:T(8,128)(2,1)S(1)}, u32[]{:S(2)}, u32[]{:S(2)}) collective-permute-start(bf16[2176,128]{1,0:T(8,128)(2,1)S(1)} %constant_dynamic-slice_fusion.6), channel_id=1, source_target_pairs={{0,2},{2,0},{4,6},{6,4},{8,10},{10,8},{12,14},{14,12},{16,18},{18,... | collective-permute-start | bytes 1671176 | tf_op jit(solution)/shard_map/ppermute | solution.py:609
  149.7 8.3 %collective-permute-start.8 = (bf16[1088,128]{1,0:T(8,128)(2,1)S(1)}, bf16[1088,128]{1,0:T(8,128)(2,1)S(1)}, u32[]{:S(2)}, u32[]{:S(2)}) collective-permute-start(bf16[1088,128]{1,0:T(8,128)(2,1)S(1)} %constant_dynamic-slice_fusion.5), channel_id=1, source_target_pairs={{0,4},{2,6},{4,0},{6,2},{8,12},{10,14},{12,8},{14,10},{16,20},{18,... | collective-permute-start | bytes 835592 | tf_op jit(solution)/shard_map/ppermute | solution.py:609
  154.2 22.9 %collective-permute-start.17 = (bf16[3840,128]{1,0:T(8,128)(2,1)S(1)}, bf16[3840,128]{1,0:T(8,128)(2,1)}, u32[]{:S(2)}, u32[]{:S(2)}) collective-permute-start(bf16[3840,128]{1,0:T(8,128)(2,1)S(1)} %pad_dynamic-slice_fusion), channel_id=1, source_target_pairs={{0,2},{2,0},{4,6},{6,4},{8,10},{10,8},{12,14},{14,12},{16,18},{18,... | collective-permute-start | bytes 2949128 | tf_op jit(solution)/shard_map/ppermute | solution.py:609
  158.1 5.1 %collective-permute-start.9 = (bf16[544,128]{1,0:T(8,128)(2,1)S(1)}, bf16[544,128]{1,0:T(8,128)(2,1)S(1)}, u32[]{:S(2)}, u32[]{:S(2)}) collective-permute-start(bf16[544,128]{1,0:T(8,128)(2,1)S(1)} %constant_dynamic-slice_fusion.4), channel_id=1, source_target_pairs={{0,8},{2,10},{4,12},{6,14},{8,0},{10,2},{12,4},{14,6},{16,24},{18,... | collective-permute-start | bytes 417800 | tf_op jit(solution)/shard_map/ppermute | solution.py:609
  163.3 16.1 %collective-permute-start.10 = (bf16[272,128]{1,0:T(8,128)(2,1)S(1)}, bf16[272,128]{1,0:T(8,128)(2,1)S(1)}, u32[]{:S(2)}, u32[]{:S(2)}) collective-permute-start(bf16[272,128]{1,0:T(8,128)(2,1)S(1)} %constant_dynamic-slice_fusion.3), channel_id=1, source_target_pairs={{0,16},{2,18},{4,20},{6,22},{8,24},{10,26},{12,28},{14,30},{16,0},... | collective-permute-start | bytes 208904 | tf_op jit(solution)/shard_map/ppermute | solution.py:609
  178.6 14.4 %copy-start.11 = (s32[4,256]{1,0:T(4,128)S(1)}, s32[4,256]{1,0:T(4,128)}, u32[]{:S(2)}) copy-start(s32[4,256]{1,0:T(4,128)} %reset.1) | copy-start | bytes 12292
  178.6 14.4 %copy-start.12 = (s32[4]{0:T(128)S(1)}, s32[4]{0:T(128)}, u32[]{:S(2)}) copy-start(s32[4]{0:T(128)} %seg_len.1) | copy-start | bytes 52
  178.7 11.4 %collective-permute-start.18 = (bf16[1920,128]{1,0:T(8,128)(2,1)S(1)}, bf16[1920,128]{1,0:T(8,128)(2,1)}, u32[]{:S(2)}, u32[]{:S(2)}) collective-permute-start(bf16[1920,128]{1,0:T(8,128)(2,1)S(1)} %constant_dynamic-slice_fusion.2), channel_id=1, source_target_pairs={{0,4},{2,6},{4,0},{6,2},{8,12},{10,14},{12,8},{14,10},{16,20},{18,... | collective-permute-start | bytes 1474568 | tf_op jit(solution)/shard_map/ppermute | solution.py:609
  179.4 5.3 %collective-permute-start.11 = (bf16[272,128]{1,0:T(8,128)(2,1)S(1)}, bf16[272,128]{1,0:T(8,128)(2,1)S(1)}, u32[]{:S(2)}, u32[]{:S(2)}) collective-permute-start(bf16[272,128]{1,0:T(8,128)(2,1)S(1)} %dynamic-slice_add_fusion.7), channel_id=1, source_target_pairs={{0,16},{2,18},{4,20},{6,22},{8,24},{10,26},{12,28},{14,30},{16,0},... | collective-permute-start | bytes 208904 | tf_op jit(solution)/shard_map/ppermute | solution.py:617
  184.7 8.4 %collective-permute-start.12 = (bf16[544,128]{1,0:T(8,128)(2,1)S(1)}, bf16[544,128]{1,0:T(8,128)(2,1)S(1)}, u32[]{:S(2)}, u32[]{:S(2)}) collective-permute-start(bf16[544,128]{1,0:T(8,128)(2,1)S(1)} %maximum_select_fusion.9), channel_id=1, source_target_pairs={{0,8},{2,10},{4,12},{6,14},{8,0},{10,2},{12,4},{14,6},{16,24},{18,... | collective-permute-start | bytes 417800 | tf_op jit(solution)/shard_map/ppermute | solution.py:617
  191.2 16.5 %copy-start.1 = (bf16[4,128,410]{1,0,2:T(4,128)(2,1)S(1)}, bf16[4,128,410]{1,0,2:T(4,128)(2,1)}, u32[]{:S(2)}) copy-start(bf16[4,128,410]{1,0,2:T(4,128)(2,1)} %param.22) | copy-start | bytes 1259524
  191.3 7.6 %collective-permute-start.19 = (bf16[960,128]{1,0:T(8,128)(2,1)S(1)}, bf16[960,128]{1,0:T(8,128)(2,1)S(1)}, u32[]{:S(2)}, u32[]{:S(2)}) collective-permute-start(bf16[960,128]{1,0:T(8,128)(2,1)S(1)} %constant_dynamic-slice_fusion.1), channel_id=1, source_target_pairs={{0,8},{2,10},{4,12},{6,14},{8,0},{10,2},{12,4},{14,6},{16,24},{18,... | collective-permute-start | bytes 737288 | tf_op jit(solution)/shard_map/ppermute | solution.py:609
  193.2 8.4 %collective-permute-start.13 = (bf16[1088,128]{1,0:T(8,128)(2,1)S(1)}, bf16[1088,128]{1,0:T(8,128)(2,1)S(1)}, u32[]{:S(2)}, u32[]{:S(2)}) collective-permute-start(bf16[1088,128]{1,0:T(8,128)(2,1)S(1)} %maximum_select_fusion.7), channel_id=1, source_target_pairs={{0,4},{2,6},{4,0},{6,2},{8,12},{10,14},{12,8},{14,10},{16,20},{18,... | collective-permute-start | bytes 835592 | tf_op jit(solution)/shard_map/ppermute | solution.py:617
  198.9 8.6 %collective-permute-start.20 = (bf16[480,128]{1,0:T(8,128)(2,1)S(1)}, bf16[480,128]{1,0:T(8,128)(2,1)S(1)}, u32[]{:S(2)}, u32[]{:S(2)}) collective-permute-start(bf16[480,128]{1,0:T(8,128)(2,1)S(1)} %constant_dynamic-slice_fusion), channel_id=1, source_target_pairs={{0,16},{2,18},{4,20},{6,22},{8,24},{10,26},{12,28},{14,30},{16,0},... | collective-permute-start | bytes 368648 | tf_op jit(solution)/shard_map/ppermute | solution.py:609
  201.8 13.1 %collective-permute-start.14 = (bf16[2176,128]{1,0:T(8,128)(2,1)S(1)}, bf16[2176,128]{1,0:T(8,128)(2,1)S(1)}, u32[]{:S(2)}, u32[]{:S(2)}) collective-permute-start(bf16[2176,128]{1,0:T(8,128)(2,1)S(1)} %maximum_select_fusion.4), channel_id=1, source_target_pairs={{0,2},{2,0},{4,6},{6,4},{8,10},{10,8},{12,14},{14,12},{16,18},{18,... | collective-permute-start | bytes 1671176 | tf_op jit(solution)/shard_map/ppermute | solution.py:617
  207.6 7.2 %collective-permute-start.21 = (bf16[480,128]{1,0:T(8,128)(2,1)S(1)}, bf16[480,128]{1,0:T(8,128)(2,1)S(1)}, u32[]{:S(2)}, u32[]{:S(2)}) collective-permute-start(bf16[480,128]{1,0:T(8,128)(2,1)S(1)} %dynamic-slice_add_fusion.6), channel_id=1, source_target_pairs={{0,16},{2,18},{4,20},{6,22},{8,24},{10,26},{12,28},{14,30},{16,0},... | collective-permute-start | bytes 368648 | tf_op jit(solution)/shard_map/ppermute | solution.py:617
  209.7 12.3 %copy-start.6 = (bf16[2,256,410]{2,1,0:T(8,128)(2,1)S(1)}, bf16[2,256,410]{2,1,0:T(8,128)(2,1)}, u32[]{:S(2)}) copy-start(bf16[2,256,410]{2,1,0:T(8,128)(2,1)} %get-tuple-element.53) | copy-start | bytes 1259524
  209.8 13.1 %collective-permute-start.5 = (bf16[2,128,410]{2,1,0:T(8,128)(2,1)S(1)}, bf16[2,128,410]{2,1,0:T(8,128)(2,1)S(1)}, u32[]{:S(2)}, u32[]{:S(2)}) collective-permute-start(bf16[2,128,410]{2,1,0:T(8,128)(2,1)S(1)} %dynamic-slice_convert_fusion), channel_id=1, source_target_pairs={{0,1},{1,0},{2,3},{3,2},{4,5},{5,4},{6,7},{7,6},{8,9},{9,8},{10,11... | collective-permute-start | bytes 629768 | tf_op jit(solution)/shard_map/ppermute | solution.py:596
  214.8 8.0 %copy-start.5 = (f32[2,256,410]{2,1,0:T(8,128)S(1)}, f32[2,256,410]{2,1,0:T(8,128)}, u32[]{:S(2)}) copy-start(f32[2,256,410]{2,1,0:T(8,128)} %get-tuple-element.59) | copy-start | bytes 2519044
  214.8 6.3 %collective-permute-start.22 = (bf16[960,128]{1,0:T(8,128)(2,1)S(1)}, bf16[960,128]{1,0:T(8,128)(2,1)S(1)}, u32[]{:S(2)}, u32[]{:S(2)}) collective-permute-start(bf16[960,128]{1,0:T(8,128)(2,1)S(1)} %maximum_select_fusion.8), channel_id=1, source_target_pairs={{0,8},{2,10},{4,12},{6,14},{8,0},{10,2},{12,4},{14,6},{16,24},{18,... | collective-permute-start | bytes 737288 | tf_op jit(solution)/shard_map/ppermute | solution.py:617
  215.2 18.2 %collective-permute-start.15 = (bf16[4352,128]{1,0:T(8,128)(2,1)S(1)}, bf16[4352,128]{1,0:T(8,128)(2,1)}, u32[]{:S(2)}, u32[]{:S(2)}) collective-permute-start(bf16[4352,128]{1,0:T(8,128)(2,1)S(1)} %maximum_select_fusion.1), channel_id=1, source_target_pairs={{0,1},{1,0},{2,3},{3,2},{4,5},{5,4},{6,7},{7,6},{8,9},{9,8},{10,11... | collective-permute-start | bytes 3342344 | tf_op jit(solution)/shard_map/ppermute | solution.py:596
  221.2 10.5 %collective-permute-start.23 = (bf16[1920,128]{1,0:T(8,128)(2,1)S(1)}, bf16[1920,128]{1,0:T(8,128)(2,1)S(1)}, u32[]{:S(2)}, u32[]{:S(2)}) collective-permute-start(bf16[1920,128]{1,0:T(8,128)(2,1)S(1)} %maximum_select_fusion.6), channel_id=1, source_target_pairs={{0,4},{2,6},{4,0},{6,2},{8,12},{10,14},{12,8},{14,10},{16,20},{18,... | collective-permute-start | bytes 1474568 | tf_op jit(solution)/shard_map/ppermute | solution.py:617
  222.8 1.9 collective-permute-start.4
  232.0 20.1 %collective-permute-start.24 = (bf16[3840,128]{1,0:T(8,128)(2,1)S(1)}, bf16[3840,128]{1,0:T(8,128)(2,1)S(1)}, u32[]{:S(2)}, u32[]{:S(2)}) collective-permute-start(bf16[3840,128]{1,0:T(8,128)(2,1)S(1)} %maximum_select_fusion.3), channel_id=1, source_target_pairs={{0,2},{2,0},{4,6},{6,4},{8,10},{10,8},{12,14},{14,12},{16,18},{18,... | collective-permute-start | bytes 2949128 | tf_op jit(solution)/shard_map/ppermute | solution.py:617
